TPU v7x, 256 devices: a whole 4x4x8 slice. The times are simulated.
256 devices in a mesh: tile: 64 (over x, z, core), chan: 4 (over y).
Axes of the slice: x: 4, y: 4, z: 8, core: 2. Of those that a mesh axis runs over, the one named last changes fastest.
Arguments:
- visibility: bfloat16 [1024, 2, 8, 512], P('tile', None, 'chan'), may hold values from -6 to 6
- imaging_weight: bfloat16 [1024, 8, 512], P('tile', 'chan'), may hold values from 0.19921875 to 5
- position: int32 [1024, 2, 512], P('tile'), may hold values from 0 to 3615
- anchor: int32 [1024, 2], P('tile'), may hold values from 0 to 128
- destination: int32 [1024], P('tile'), may hold values from 0 to 63, as said below
- block_count: int32 [64], P('tile'), may hold values from 12 to 16, as said below
- kernel: float32 [32, 16], replicated, may hold values from 0.25 to 1.5
Outputs:
- combined_grid: float32 [2, 16384, 256], P(None, ('tile', 'chan'))
- residual: bfloat16 [1024, 2, 8, 512], P('tile', None, 'chan')
Inputs may be any that keep to these rules, and one draw needn't show every extreme that they name: `destination`: among each owner's 16 blocks at most 2 name one tile; one tile is named by exactly 2 blocks of every owner, all of them among that owner's first 8 blocks. Owner i's live blocks are its first block_count[i]; some owner has all 16 live. `position`: every entry is below 2^12. A program may carry positions, corners and other integer fields packed into fewer bits when they are sent, as long as nothing is lost.
All inputs are finite; a program needn't handle non-finite values.
Results may differ from a plain program's by a relative error of at most 0.009.
Values may be sent and summed in bfloat16 or wider, within the bound.
A program may use at most 64 MiB of HBM per device.

v0:
```python
import jax
import jax.numpy as jnp
from jax import lax
from jax.sharding import PartitionSpec as P

TAPS = 16
OS = 32
SUB = 128
TS = 256


turn_blocks = 8


def from_partner(block, axis, apart):
    count = lax.axis_size(axis)
    route = []
    for low in range(count):
        high = low | 1 << apart
        if high != low and high < count:
            route += [(low, high), (high, low)]
    return lax.ppermute(block, axis, route)


def tap_block(positions, kernel, across):
    cell_row = positions // OS
    offset = positions % OS
    chosen = (offset[:, None, :] == jnp.arange(OS, dtype=jnp.int32)[None, :, None]).astype(
        jnp.float32
    )
    tap_values = jnp.einsum("gov,ok->gkv", chosen, kernel, precision=lax.Precision.HIGHEST)
    cell_ids = jnp.arange(SUB, dtype=jnp.int32)
    if across:
        distance = cell_ids[None, None, :] - cell_row[:, :, None]
    else:
        distance = cell_ids[None, :, None] - cell_row[:, None, :]
    matrix = jnp.zeros(distance.shape, jnp.float32)
    for tap_index in range(TAPS):
        tap_row = tap_values[:, tap_index]
        spread = tap_row[:, :, None] if across else tap_row[:, None, :]
        matrix = matrix + jnp.where(distance == tap_index, spread, jnp.float32(0.0))
    return matrix.astype(jnp.bfloat16)


def grid_items(tile_grid, values, weights, positions, corner, usable, mirrored, kernel):
    channels = values.shape[2]
    row_taps = tap_block(positions[:, 0], kernel, False)
    col_taps = tap_block(positions[:, 1], kernel, True)
    scaled = values.astype(jnp.float32) * weights.astype(jnp.float32)[:, None]
    weighted = (scaled[..., None] * col_taps.astype(jnp.float32)[:, None, None]).astype(
        jnp.bfloat16
    )
    patches = jnp.einsum("giv,grcvj->grcij", row_taps, weighted, preferred_element_type=jnp.float32)
    conj_sign = jnp.array([1.0, -1.0], jnp.float32).reshape(1, 2, 1, 1, 1)
    turned = patches[..., ::-1, ::-1] * conj_sign
    patches = jnp.where(mirrored[:, None, None, None, None], turned, patches)
    patches = jnp.where(usable[:, None, None, None, None], patches, jnp.float32(0.0))
    corner = jnp.where(mirrored[:, None], TS - SUB - corner, corner)
    for item in range(values.shape[0]):
        start_at = (jnp.int32(0), jnp.int32(0), corner[item, 0], corner[item, 1])
        current = lax.dynamic_slice(tile_grid, start_at, (2, channels, SUB, SUB))
        tile_grid = lax.dynamic_update_slice(tile_grid, current + patches[item], start_at)
    return tile_grid


def degrid_items(symmetric, positions, corner, usable, mirrored, kernel):
    channels = symmetric.shape[1]
    row_taps = tap_block(positions[:, 0], kernel, False)
    col_taps = tap_block(positions[:, 1], kernel, True)
    corner = jnp.where(mirrored[:, None], TS - SUB - corner, corner)
    pieces = []
    for item in range(positions.shape[0]):
        start_at = (jnp.int32(0), jnp.int32(0), corner[item, 0], corner[item, 1])
        pieces.append(lax.dynamic_slice(symmetric, start_at, (2, channels, SUB, SUB)))
    window = jnp.stack(pieces)
    conj_sign = jnp.array([1.0, -1.0], jnp.float32).reshape(1, 2, 1, 1, 1)
    turned = window[..., ::-1, ::-1] * conj_sign
    window = jnp.where(mirrored[:, None, None, None, None], turned, window).astype(jnp.bfloat16)
    product = jnp.einsum("giv,grcij->grcvj", row_taps, window, preferred_element_type=jnp.float32)
    predicted = jnp.sum(product * col_taps.astype(jnp.float32)[:, None, None], axis=-1) / (
        TAPS * TAPS
    )
    return jnp.where(usable[:, None, None, None], predicted, jnp.float32(0.0)).astype(jnp.bfloat16)


def complete_grid(tile_grid, mirror_bit):
    conj_sign = jnp.array([1.0, -1.0], jnp.float32).reshape(2, 1, 1, 1)
    partner_grid = from_partner(tile_grid, "tile", mirror_bit)
    return tile_grid + partner_grid[:, :, ::-1, ::-1] * conj_sign


def per_device(visibility, imaging_weight, position, anchor, destination, block_count, kernel):
    tile_count = lax.axis_size("tile")
    mirror_bit = tile_count.bit_length() - 2
    owned_blocks = visibility.shape[0]
    channels = visibility.shape[2]
    block_width = visibility.shape[3]
    bucket = max(2, 2 * owned_blocks // tile_count)
    slot_total = tile_count * bucket
    block_ids = jnp.arange(owned_blocks, dtype=jnp.int32)
    is_live = block_ids < block_count[0]
    same_tile = destination[:, None] == destination[None, :]
    earlier = block_ids[None, :] < block_ids[:, None]
    rank_in_tile = jnp.sum((same_tile & earlier).astype(jnp.int32), axis=1)
    slot_of = destination * bucket + rank_in_tile
    slot_ids = jnp.arange(slot_total, dtype=jnp.int32)
    matches = slot_of[None, :] == slot_ids[:, None]
    filled = jnp.any(matches, axis=1)
    source = jnp.sum(jnp.where(matches, block_ids[None, :], 0), axis=1)
    send_values = jnp.where(
        filled[:, None, None, None], visibility[source], jnp.zeros((), jnp.bfloat16)
    )
    send_weights = jnp.where(
        filled[:, None, None], imaging_weight[source], jnp.zeros((), jnp.bfloat16)
    )
    send_positions = jnp.where(filled[:, None, None], position[source], 0)
    send_corner = jnp.where(filled[:, None], anchor[source], 0)
    send_live = (filled & is_live[source]).astype(jnp.int32)
    got_values, got_weights = (
        lax.all_to_all(send_values, "tile", split_axis=0, concat_axis=0, tiled=True),
        lax.all_to_all(send_weights, "tile", split_axis=0, concat_axis=0, tiled=True),
    )
    got_positions, got_corner, got_live = (
        lax.all_to_all(send_positions, "tile", split_axis=0, concat_axis=0, tiled=True),
        lax.all_to_all(send_corner, "tile", split_axis=0, concat_axis=0, tiled=True),
        lax.all_to_all(send_live, "tile", split_axis=0, concat_axis=0, tiled=True),
    )
    sort_key = (1 - got_live) * slot_total + slot_ids
    ordering = jnp.argsort(sort_key)
    back_order = jnp.argsort(ordering)
    live_count = jnp.sum(got_live)
    packed_values = got_values[ordering]
    packed_weights = got_weights[ordering]
    packed_positions = got_positions[ordering]
    packed_corner = got_corner[ordering]
    step_ids = jnp.arange(turn_blocks, dtype=jnp.int32)
    tile_grid = jnp.zeros((2, channels, TS, TS), jnp.float32)
    no_mirror = jnp.zeros((turn_blocks,), bool)
    own_turns = (live_count + turn_blocks - 1) // turn_blocks

    def grid_turn(turn, grid_now):
        start_row = turn * turn_blocks
        usable = start_row + step_ids < live_count
        return grid_items(
            grid_now,
            lax.dynamic_slice_in_dim(packed_values, start_row, turn_blocks, 0),
            lax.dynamic_slice_in_dim(packed_weights, start_row, turn_blocks, 0),
            lax.dynamic_slice_in_dim(packed_positions, start_row, turn_blocks, 0),
            lax.dynamic_slice_in_dim(packed_corner, start_row, turn_blocks, 0),
            usable,
            no_mirror,
            kernel,
        )

    tile_grid = lax.fori_loop(jnp.int32(0), own_turns, grid_turn, tile_grid)
    symmetric = complete_grid(tile_grid, mirror_bit)

    def degrid_turn(turn, results):
        start_row = turn * turn_blocks
        usable = start_row + step_ids < live_count
        predicted = degrid_items(
            symmetric,
            lax.dynamic_slice_in_dim(packed_positions, start_row, turn_blocks, 0),
            lax.dynamic_slice_in_dim(packed_corner, start_row, turn_blocks, 0),
            usable,
            no_mirror,
            kernel,
        )
        return lax.dynamic_update_slice_in_dim(results, predicted, start_row, 0)

    results = jnp.zeros((slot_total, 2, channels, block_width), jnp.bfloat16)
    own_results = lax.fori_loop(jnp.int32(0), own_turns, degrid_turn, results)
    combined_grid = lax.psum_scatter(
        jnp.sum(symmetric, axis=1), "chan", scatter_dimension=1, tiled=True
    )
    slot_results = own_results[back_order]
    returned_slots = lax.all_to_all(slot_results, "tile", split_axis=0, concat_axis=0, tiled=True)
    returned = jnp.where(
        is_live[:, None, None, None], returned_slots[slot_of], jnp.zeros((), jnp.bfloat16)
    )
    residual = (visibility.astype(jnp.float32) - returned.astype(jnp.float32)).astype(jnp.bfloat16)
    return (combined_grid, residual)


def solution(mesh):
    placed = (
        P("tile", None, "chan", None),
        P("tile", "chan", None),
        P("tile", None, None),
        P("tile", None),
        P("tile"),
        P("tile"),
        P(),
    )
    return jax.shard_map(
        per_device,
        mesh=mesh,
        in_specs=placed,
        out_specs=(P(None, ("tile", "chan"), None), P("tile", None, "chan", None)),
        check_vma=False,
    )
```

profile of v0, /device:TPU:1, one launch (start us, length us, event | category | flops | bytes accessed | tf_op | source)
XLA Modules:
  0.0 2303.2 jit_solution(3588358292816547618)
XLA Ops:
  8.1 1.2 compare_select_fusion
  11.4 9.8 fusion.235
  22.0 13.0 all-to-all-start
  37.4 1.9 gather_fusion.4
  39.3 5.0 all-to-all-done
  44.3 5.4 all-to-all-start.1
  50.7 8.7 all-to-all-done.1
  59.4 4.4 all-to-all-start.3
  66.1 9.8 all-to-all-done.3
  75.9 6.1 all-to-all-start.4
  82.0 1.6 gather_fusion.2
  83.7 1.3 broadcast_select_fusion
  85.0 14.3 all-to-all-done.4
  99.3 18.2 all-to-all-start.2
  119.1 2.6 sort.31
  122.3 1.1 gather_fusion.5
  125.6 9.2 all-to-all-done.2
  134.7 1.6 gather_fusion.3
  136.5 152.6 %while.30 = (s32[]{:T(128)}, f32[2,2,256,256]{2,3,1,0:T(8,128)S(1)}, s32[]{:T(128)}, s32[128,2]{0,1:T(2,128)S(1)}, s32[]{:T(128)}, /*index=5*/bf16[128,2,2,512]{...) while((s32[]{:T(128)}, ...), condition=%wide.region_6.7_spmd.clone, body=%wide.region_5.6_spmd.clone.sunk | while | flops 644861952 | bytes 35058928 | solution.py:155
  139.4 3.5 fusion.291
  144.3 5.1 select_bitcast_fusion.2
  154.3 3.2 dynamic_update_slice.91
  162.2 3.2 dynamic_update_slice.92
  170.2 3.1 dynamic_update_slice.93
  178.2 3.3 dynamic_update_slice.94
  186.3 3.4 dynamic_update_slice.95
  194.4 3.3 dynamic_update_slice.96
  202.8 3.3 dynamic_update_slice.97
  210.9 3.0 dynamic_update_slice.98
  216.9 3.5 fusion.291
  221.8 5.1 select_bitcast_fusion.2
  231.8 3.4 dynamic_update_slice.91
  240.0 3.2 dynamic_update_slice.92
  248.0 3.1 dynamic_update_slice.93
  256.0 3.3 dynamic_update_slice.94
  264.1 3.2 dynamic_update_slice.95
  272.1 3.3 dynamic_update_slice.96
  280.4 1.8 dynamic_update_slice.97
  287.0 1.8 dynamic_update_slice.98
  289.2 2.5 sort.32
  291.8 12.6 collective-permute-done
  304.4 1.4 rev.3
  307.1 104.8 %while.31 = (s32[]{:T(128)}, bf16[128,2,2,512]{3,2,1,0:T(2,128)(2,1)S(1)}, s32[]{:T(128)}, s32[]{:T(128)}, s32[128,2]{0,1:T(2,128)S(1)}, /*index=5*/bf16[2,2,256...) while((s32[]{:T(128)}, ...), condition=%wide.region_11.12_spmd.clone, body=%wide.region_9.11_spmd.clone.sunk | while | flops 643805184 | bytes 10860107 | solution.py:172
  316.6 1.1 fusion.313
  321.9 1.1 fusion.314
  326.5 1.1 fusion.315
  331.4 1.1 fusion.316
  336.2 1.1 fusion.317
  341.1 1.1 fusion.318
  345.6 1.1 fusion.319
  349.6 3.5 fusion.310
  353.7 5.0 fusion.321
  369.0 1.1 fusion.313
  374.3 1.1 fusion.314
  378.9 1.1 fusion.315
  383.8 1.1 fusion.316
  388.6 1.1 fusion.317
  393.5 1.1 fusion.318
  398.0 1.1 fusion.319
  402.0 3.5 fusion.310
  406.1 5.0 fusion.321
  411.9 2.4 gather_fusion.8
  414.3 1827.9 %all-to-all-start.5 = ((bf16[128,2,2,512]{3,2,1,0:T(2,128)(2,1)}), bf16[128,2,2,512]{3,2,1,0:T(2,128)(2,1)S(1)}, u32[]{:S(2)}, u32[]{:S(2)}) async-start(bf16[128,2,2,512]{3,2,1,0:T(2,128)(2,1)} %gather_fusion.8), calls=%async_computation.5 | async-start | bytes 1048576 | tf_op jit(solution)/shard_map/all_to_all | solution.py:177
  2244.7 48.2 %all-reduce.3.cloned.1.call-done = f32[2,256,256]{2,0,1:T(2,128)} async-done(((f32[2,256,256]{2,0,1:T(2,128)}), f32[2,256,256]{2,0,1:T(2,128)}) %all-reduce.3.cloned.1.call-update) | async-done | bytes 524304
  (209 shorter events, 56.4 us)
Async XLA Ops:
  7.2 56.7 %copy-start = (s32[16,2,512]{2,1,0:T(2,128)S(1)}, s32[16,2,512]{2,1,0:T(2,128)}, u32[]{:S(2)}) copy-start(s32[16,2,512]{2,1,0:T(2,128)} %param.14) | copy-start | bytes 196612
  10.2 0.6 copy-start.9
  22.0 22.2 all-to-all-start
  44.3 15.2 all-to-all-start.1
  49.6 32.4 %copy-start.2 = (bf16[16,2,2,512]{3,2,1,0:T(2,128)(2,1)S(1)}, bf16[16,2,2,512]{3,2,1,0:T(2,128)(2,1)}, u32[]{:S(2)}) copy-start(bf16[16,2,2,512]{3,2,1,0:T(2,128)(2,1)} %param.12) | copy-start | bytes 196612
  59.4 16.5 all-to-all-start.3
  75.9 23.4 %all-to-all-start.4 = ((s32[128,2,512]{2,1,0:T(2,128)}), s32[128,2,512]{2,1,0:T(2,128)S(1)}, u32[]{:S(2)}, u32[]{:S(2)}) async-start(s32[128,2,512]{2,1,0:T(2,128)} %broadcast_select_fusion.1), calls=%async_computation.4 | async-start | bytes 1048576 | tf_op jit(solution)/shard_map/all_to_all | solution.py:124
  99.3 35.4 %all-to-all-start.2 = ((bf16[128,2,2,512]{3,2,1,0:T(2,128)(2,1)}), bf16[128,2,2,512]{3,2,1,0:T(2,128)(2,1)S(1)}, u32[]{:S(2)}, u32[]{:S(2)}) async-start(bf16[128,2,2,512]{3,2,1,0:T(2,128)(2,1)} %broadcast_select_fusion), calls=%async_computation.2 | async-start | bytes 1048576 | tf_op jit(solution)/shard_map/all_to_all | solution.py:120
  123.5 12.9 copy-start.4
  136.5 7.1 copy-start.7
  136.5 7.1 copy-start.5
  149.4 11.7 copy-start.1
  189.6 24.3 %copy-start.6 = (bf16[128,2,2,512]{3,2,1,0:T(2,128)(2,1)S(1)}, bf16[128,2,2,512]{3,2,1,0:T(2,128)(2,1)}, u32[]{:S(2)}) copy-start(bf16[128,2,2,512]{3,2,1,0:T(2,128)(2,1)} %copy-done.5) | copy-start | bytes 1572868 | tf_op jit(solution)/shard_map/while
  189.6 24.3 %copy-start.8 = (bf16[128,2,512]{2,1,0:T(2,128)(2,1)S(1)}, bf16[128,2,512]{2,1,0:T(2,128)(2,1)}, u32[]{:S(2)}) copy-start(bf16[128,2,512]{2,1,0:T(2,128)(2,1)} %copy-done.7) | copy-start | bytes 786436 | tf_op jit(solution)/shard_map/while
  214.0 7.1 copy-start.7
  214.0 7.1 copy-start.5
  226.9 11.9 copy-start.1
  267.3 21.6 copy-start.6
  267.3 21.6 copy-start.8
  289.1 16.7 copy-start.12
  289.1 15.2 collective-permute-start
  414.3 1829.1 %copy-start.13 = (u32[256]{0:T(256)S(1)}, u32[256]{0:T(256)}, u32[]{:S(2)}) copy-start(u32[256]{0:T(256)} %constant.510) | copy-start | bytes 3076
  414.3 1830.4 %copy-start.11 = (s32[16]{0:T(128)S(1)}, s32[16]{0:T(128)}, u32[]{:S(2)}) copy-start(s32[16]{0:T(128)} %get-tuple-element.541) | copy-start | bytes 196
  414.3 1880.2 %all-to-all-start.5 = ((bf16[128,2,2,512]{3,2,1,0:T(2,128)(2,1)}), bf16[128,2,2,512]{3,2,1,0:T(2,128)(2,1)S(1)}, u32[]{:S(2)}, u32[]{:S(2)}) async-start(bf16[128,2,2,512]{3,2,1,0:T(2,128)(2,1)} %gather_fusion.8), calls=%async_computation.5 | async-start | bytes 1048576 | tf_op jit(solution)/shard_map/all_to_all | solution.py:177
  2242.2 53.0 %copy-start.3 = (bf16[16,2,2,512]{3,2,1,0:T(2,128)(2,1)S(1)}, bf16[16,2,2,512]{3,2,1,0:T(2,128)(2,1)}, u32[]{:S(2)}) copy-start(bf16[16,2,2,512]{3,2,1,0:T(2,128)(2,1)} %param.12) | copy-start | bytes 196612
  2242.2 53.0 %copy-start.10 = (pred[16]{0:T(512)(128)(4,1)S(1)}, pred[16]{0:T(512)(128)(4,1)}, u32[]{:S(2)}) copy-start(pred[16]{0:T(512)(128)(4,1)} %copy-done.9) | copy-start | bytes 52
  2242.2 50.7 %all-reduce.3.cloned.1.call-start = ((), (), s32[]{:S(2)}) async-start(), calls=%async_computation.6 | async-start | bytes 1048576
Sparse Core Ops, SparseCore 0:
  2245.4 47.4 all-reduce.2
where the time goes:
time: 2340 us; the launch traced here: 2300 us
  starting transfers between devices  1880 us (80%)
  loops' own time  120 us (5%)
  waiting for transfers between devices  108 us (5%)
  local copies, waits for them, and re-layouts  94.9 us (4%)
  other arithmetic  65.7 us (3%)
    all_to_all x1, starting transfers between devices, per_device(): lax.all_to_all(slot_results, 'tile', split_axis=0, concat_axis=0, tiled=T...  1830 us
    another operation x1, loops' own time, per_device(): tile_grid = lax.fori_loop(jnp.int32(0), own_turns, grid_turn, tile_grid)  60.6 us
    another operation x1, loops' own time, per_device(): own_results = lax.fori_loop(jnp.int32(0), own_turns, degrid_turn, results)  59.9 us
    dynamic_update_slice x16, local copies, waits for them, and re-layouts, grid_items(): lax.dynamic_update_slice(tile_grid, current + patches[item], start_at)  49 us
    unnamed x2, waiting for transfers between devices  48.2 us
  transfers between devices with their start and end apart: 8, of which 7 were waited for; matrix products, arithmetic and copies ran while one was open for 1% of the time, Pallas kernels for 0%

commit v1 on v0

v1 whole, which is shorter than its diff:
```python
import functools

import jax
import jax.numpy as jnp
from jax import lax
from jax.experimental import pallas as pl
from jax.experimental.pallas import tpu as pltpu
from jax.sharding import PartitionSpec as P

TAPS = 16
OS = 32
SUB = 128
TS = 256
TILES = 64
CHAN = 4
SLOTS = 128
ROWS = 144
GROUPS = 4
LIMIT = 40 * 1024 * 1024

VMEM = pl.BlockSpec(memory_space=pltpu.VMEM)
SMEM = pl.BlockSpec(memory_space=pltpu.SMEM)
MESH = pl.DeviceIdType.MESH


def sort_kernel(dest, count, anchor, vis, weight, pos, scaled, packed, info, used):
    me = lax.axis_index("tile")
    turn = me + (me >> 2) + (me >> 4)
    scaled[...] = jnp.zeros(scaled.shape, scaled.dtype)
    packed[...] = jnp.zeros(packed.shape, packed.dtype)
    for quad in range(TILES // 4):
        used[quad] = 0
    half = lax.broadcasted_iota(jnp.int32, (8, 128), 0) // GROUPS
    for b in range(16):
        alive = (b < count[0]).astype(jnp.int32)
        tile = dest[b]
        quad = (tile & 31) >> 1
        rank = used[quad]
        used[quad] = rank + alive
        member = (rank + turn) & 3
        device = (quad << 1) | (member & 1) | ((member >> 1) << 5)
        which = rank >> 2
        mirror = tile >> 5
        flip = 1 - 2 * mirror
        top = mirror * (TS - SUB) + flip * anchor[2 * b]
        left = mirror * (TS - SUB) + flip * anchor[2 * b + 1]
        base = jnp.minimum(top >> 4, 7)
        info[b] = (device * 2 + which) | (mirror << 8) | (alive << 9)
        meta = (alive << 26) | (base << 27) | (mirror << 30) | ((tile & 1) << 31)

        @pl.when(alive == 1)
        def _():
            place = pos[b]
            cell = mirror * (SUB - TAPS) + flip * (place >> 5)
            offset = place & (OS - 1)
            row = (cell[:4] + (top - base * 16)) * OS + offset[:4]
            column = (cell[4:] + left) * OS + offset[4:]
            word = row | (column << 13) | meta
            both = jnp.concatenate([word, word], axis=0)
            packed[device] = jnp.where(half == which, both, packed[device])
            values = vis[b].astype(jnp.float32)
            factor = weight[b].astype(jnp.float32)
            sign = flip.astype(jnp.float32)
            scaled[device * 2 + which] = jnp.concatenate(
                [values[:8] * factor, values[8:] * factor * sign], axis=0
            ).astype(jnp.bfloat16)


def sort_blocks(dest, count, anchor, vis, weight, pos):
    return pl.pallas_call(
        sort_kernel,
        out_shape=(
            jax.ShapeDtypeStruct((SLOTS, 16, 128), jnp.bfloat16),
            jax.ShapeDtypeStruct((TILES, 8, 128), jnp.int32),
            jax.ShapeDtypeStruct((16,), jnp.int32),
        ),
        in_specs=[SMEM, SMEM, SMEM, VMEM, VMEM, VMEM],
        out_specs=(VMEM, VMEM, SMEM),
        scratch_shapes=[pltpu.SMEM((TILES // 4,), jnp.int32)],
        name="sort_blocks",
    )(dest, count, anchor, vis, weight, pos)


def greet_tiles(me):
    barrier = pltpu.get_barrier_semaphore()

    def greet(step, carry):
        pl.semaphore_signal(
            barrier, inc=1, device_id={"tile": (me + step) % TILES}, device_id_type=MESH
        )
        return carry

    lax.fori_loop(1, TILES, greet, 0)
    return barrier


def route_kernel(scaled, packed, got_scaled, got_packed, s_out, s_in, p_out, p_in, here):
    me = lax.axis_index("tile")
    pl.semaphore_wait(greet_tiles(me), TILES - 1)

    def copies(peer):
        first = pltpu.make_async_remote_copy(
            src_ref=scaled.at[pl.ds(peer * 2, 2)],
            dst_ref=got_scaled.at[pl.ds(me * 2, 2)],
            send_sem=s_out.at[peer],
            recv_sem=s_in.at[me],
            device_id={"tile": peer},
            device_id_type=MESH,
        )
        second = pltpu.make_async_remote_copy(
            src_ref=packed.at[pl.ds(peer, 1)],
            dst_ref=got_packed.at[pl.ds(me, 1)],
            send_sem=p_out.at[peer],
            recv_sem=p_in.at[me],
            device_id={"tile": peer},
            device_id_type=MESH,
        )
        return first, second

    def send(step, carry):
        first, second = copies((me + step) % TILES)
        first.start()
        second.start()
        return carry

    lax.fori_loop(1, TILES, send, 0)
    own_scaled = pltpu.make_async_copy(
        scaled.at[pl.ds(me * 2, 2)], got_scaled.at[pl.ds(me * 2, 2)], here.at[0]
    )
    own_packed = pltpu.make_async_copy(
        packed.at[pl.ds(me, 1)], got_packed.at[pl.ds(me, 1)], here.at[1]
    )
    own_scaled.start()
    own_packed.start()
    own_scaled.wait()
    own_packed.wait()

    def finish(step, carry):
        peer = (me + step) % TILES
        pltpu.make_async_copy(
            got_scaled.at[pl.ds(peer * 2, 2)], got_scaled.at[pl.ds(peer * 2, 2)], s_in.at[peer]
        ).wait()
        pltpu.make_async_copy(
            got_packed.at[pl.ds(peer, 1)], got_packed.at[pl.ds(peer, 1)], p_in.at[peer]
        ).wait()
        first, second = copies(peer)
        first.wait_send()
        second.wait_send()
        return carry

    lax.fori_loop(1, TILES, finish, 0)


def route(scaled, packed):
    return pl.pallas_call(
        route_kernel,
        out_shape=(
            jax.ShapeDtypeStruct(scaled.shape, scaled.dtype),
            jax.ShapeDtypeStruct(packed.shape, packed.dtype),
        ),
        in_specs=[VMEM, VMEM],
        out_specs=(VMEM, VMEM),
        scratch_shapes=[pltpu.SemaphoreType.DMA((TILES,))] * 4 + [pltpu.SemaphoreType.DMA((2,))],
        compiler_params=pltpu.CompilerParams(
            collective_id=0, has_side_effects=True, vmem_limit_bytes=LIMIT
        ),
        name="route",
    )(scaled, packed)


def gather_live(meta, order):
    def look(slot, count):
        order[count] = slot
        return count + ((meta[slot] >> 26) & 1)

    count = lax.fori_loop(0, SLOTS, look, jnp.int32(0))
    return count


def tap_rows(table, cell, column, pieces):
    cell = jnp.broadcast_to(cell, (8, 128))
    column = jnp.broadcast_to(column, (8, 128))
    low = jnp.take_along_axis(table[:8], column, axis=1, mode="promise_in_bounds")
    high = jnp.take_along_axis(table[8:], column, axis=1, mode="promise_in_bounds")
    sub = lax.broadcasted_iota(jnp.int32, (8, 128), 0)
    part = cell & 7
    whole = cell >> 3
    turn = (sub - part) & 7
    low = jnp.take_along_axis(low, turn, axis=0, mode="promise_in_bounds")
    high = jnp.take_along_axis(high, turn, axis=0, mode="promise_in_bounds")
    after = sub >= part
    zero = jnp.zeros((8, 128), jnp.float32)
    first = jnp.where(after, low, zero)
    second = jnp.where(after, high, low)
    third = jnp.where(after, zero, high)
    at = [whole == m for m in range(pieces)]
    rows = []
    for m in range(pieces):
        value = zero
        if m >= 2:
            value = jnp.where(at[m - 2], third, value)
        if m >= 1:
            value = jnp.where(at[m - 1], second, value)
        rows.append(jnp.where(at[m], first, value))
    return jnp.concatenate(rows, axis=0)


def slot_taps(packed, table, slot, word):
    both = packed[slot >> 1]
    mine = jnp.where((slot & 1) == 1, both[4:], both[:4])
    shift = OS * ((word >> 30) & 1)
    row_cell = (mine >> 5) & 255
    row_column = (mine & (OS - 1)) + shift
    col_cell = (mine >> 18) & 255
    col_column = ((mine >> 13) & (OS - 1)) + shift
    rows = [
        tap_rows(table, row_cell[g : g + 1], row_column[g : g + 1], ROWS // 8)
        for g in range(GROUPS)
    ]
    cols = [
        tap_rows(table, col_cell[g : g + 1], col_column[g : g + 1], TS // 8).astype(jnp.bfloat16)
        for g in range(GROUPS)
    ]
    return rows, jnp.concatenate(cols, axis=1)


def grid_kernel(meta, scaled, packed, table, grid, order):
    count = gather_live(meta, order)
    grid[...] = jnp.zeros(grid.shape, grid.dtype)
    taps = table[...]

    def one(slot, keep):
        word = meta[slot]
        rows, cols = slot_taps(packed, taps, slot, word)
        values = scaled[slot].astype(jnp.float32) * keep
        planes = []
        for plane in range(4):
            parts = [
                (rows[g] * values[plane * GROUPS + g : plane * GROUPS + g + 1]).astype(jnp.bfloat16)
                for g in range(GROUPS)
            ]
            planes.append(jnp.concatenate(parts, axis=1))
        left = jnp.concatenate(planes, axis=0)
        product = lax.dot_general(
            left, cols, (((1,), (1,)), ((), ())), preferred_element_type=jnp.float32
        )
        which = (word >> 31) & 1
        start = pl.multiple_of(((word >> 27) & 7) * 16, 16)
        for plane in range(4):
            grid[which, plane, pl.ds(start, ROWS), :] += product[plane * ROWS : (plane + 1) * ROWS]

    def step(turn, carry):
        one(order[2 * turn], jnp.float32(1.0))
        later = 2 * turn + 1
        extra = later < count
        one(order[jnp.where(extra, later, 0)], extra.astype(jnp.float32))
        return carry

    lax.fori_loop(0, (count + 1) >> 1, step, 0)


def grid_blocks(meta, scaled, packed, table):
    return pl.pallas_call(
        grid_kernel,
        out_shape=jax.ShapeDtypeStruct((2, 4, TS, TS), jnp.float32),
        in_specs=[SMEM, VMEM, VMEM, VMEM],
        out_specs=VMEM,
        scratch_shapes=[pltpu.SMEM((SLOTS + 8,), jnp.int32)],
        compiler_params=pltpu.CompilerParams(vmem_limit_bytes=LIMIT),
        name="grid_blocks",
    )(meta, scaled, packed, table)


def join_kernel(grid, whole, summed, half, got_half, total, mine, got_mine, send, recv):
    me = lax.axis_index("tile")
    core = me & 1
    near = me ^ 1
    far = me ^ (TILES // 2)
    barrier = pltpu.get_barrier_semaphore()
    for peer in (near, far):
        pl.semaphore_signal(barrier, inc=1, device_id={"tile": peer}, device_id_type=MESH)

    def pass_on(source, target, sem, peer):
        return pltpu.make_async_remote_copy(
            src_ref=source,
            dst_ref=target,
            send_sem=send.at[sem],
            recv_sem=recv.at[sem],
            device_id={"tile": peer},
            device_id_type=MESH,
        )

    pl.semaphore_wait(barrier, 2)
    first = [pass_on(half.at[k], got_half.at[k], k, near) for k in range(4)]
    second = [pass_on(mine.at[k], got_mine.at[k], 4 + k, far) for k in range(4)]
    third = [pass_on(whole.at[core, k], whole.at[core, k], 8 + k, near) for k in range(4)]
    for k in range(4):
        half[k] = grid[1 - core, k].astype(jnp.bfloat16)
        first[k].start()
    for k in range(4):
        first[k].wait_recv()
        value = grid[core, k] + got_half[k].astype(jnp.float32)
        total[k] = value
        mine[k] = value.astype(jnp.bfloat16)
        second[k].start()
    for k in range(4):
        second[k].wait_recv()
        value = total[k] + got_mine[k].astype(jnp.float32)
        whole[core, k] = value.astype(jnp.bfloat16)
        third[k].start()
        if k % 2 == 0:
            summed[k // 2] = value
        else:
            summed[k // 2] += value
    for k in range(4):
        other = pltpu.make_async_copy(whole.at[1 - core, k], whole.at[1 - core, k], recv.at[8 + k])
        other.wait()
        first[k].wait_send()
        second[k].wait_send()
        third[k].wait_send()


def join_grids(grid):
    return pl.pallas_call(
        join_kernel,
        out_shape=(
            jax.ShapeDtypeStruct((2, 4, TS, TS), jnp.bfloat16),
            jax.ShapeDtypeStruct((2, TS, TS), jnp.float32),
        ),
        in_specs=[VMEM],
        out_specs=(VMEM, VMEM),
        scratch_shapes=[
            pltpu.VMEM((4, TS, TS), jnp.bfloat16),
            pltpu.VMEM((4, TS, TS), jnp.bfloat16),
            pltpu.VMEM((4, TS, TS), jnp.float32),
            pltpu.VMEM((4, TS, TS), jnp.bfloat16),
            pltpu.VMEM((4, TS, TS), jnp.bfloat16),
            pltpu.SemaphoreType.DMA((12,)),
            pltpu.SemaphoreType.DMA((12,)),
        ],
        compiler_params=pltpu.CompilerParams(
            collective_id=1, has_side_effects=True, vmem_limit_bytes=LIMIT
        ),
        name="join_grids",
    )(grid)


def degrid_kernel(meta, packed, table, whole, predicted, order):
    count = gather_live(meta, order)
    taps = table[...]

    def one(slot):
        word = meta[slot]
        rows, cols = slot_taps(packed, taps, slot, word)
        which = (word >> 31) & 1
        start = pl.multiple_of(((word >> 27) & 7) * 16, 16)
        results = []
        for plane in range(4):
            window = whole[which, plane, pl.ds(start, ROWS), :]
            across = jnp.dot(window, cols, preferred_element_type=jnp.float32)
            for g in range(GROUPS):
                results.append(
                    jnp.sum(rows[g] * across[:, g * 128 : (g + 1) * 128], axis=0, keepdims=True)
                )
        scale = jnp.float32(1.0 / (TAPS * TAPS))
        predicted[slot] = (jnp.concatenate(results, axis=0) * scale).astype(jnp.bfloat16)

    def step(turn, carry):
        one(order[2 * turn])
        later = 2 * turn + 1
        one(order[jnp.where(later < count, later, 0)])
        return carry

    lax.fori_loop(0, (count + 1) >> 1, step, 0)


def degrid_blocks(meta, packed, table, whole):
    return pl.pallas_call(
        degrid_kernel,
        out_shape=jax.ShapeDtypeStruct((SLOTS, 16, 128), jnp.bfloat16),
        in_specs=[SMEM, VMEM, VMEM, VMEM],
        out_specs=VMEM,
        scratch_shapes=[pltpu.SMEM((SLOTS + 8,), jnp.int32)],
        compiler_params=pltpu.CompilerParams(vmem_limit_bytes=LIMIT),
        name="degrid_blocks",
    )(meta, packed, table, whole)


def back_kernel(
    info, predicted, vis, summed, residual, combined, back, parts, b_out, b_in, c_out, c_in, here
):
    me = lax.axis_index("tile")
    chan = lax.axis_index("chan")
    upper = me // (TILES // 2)
    barrier = greet_tiles(me)
    for k in range(1, CHAN):
        pl.semaphore_signal(
            barrier, inc=1, device_id={"chan": (chan + k) % CHAN}, device_id_type=MESH
        )
    pl.semaphore_wait(barrier, TILES - 1 + CHAN - 1)

    def rows_of(group):
        place = group + upper * (CHAN - 1 - 2 * group)
        return pl.ds(pl.multiple_of(place * (TS // CHAN), TS // CHAN), TS // CHAN)

    def across(k):
        group = (chan + k) % CHAN
        return pltpu.make_async_remote_copy(
            src_ref=summed.at[:, rows_of(group), :],
            dst_ref=parts.at[k - 1],
            send_sem=c_out.at[k - 1],
            recv_sem=c_in.at[k - 1],
            device_id={"chan": group},
            device_id_type=MESH,
        )

    def home(peer):
        return pltpu.make_async_remote_copy(
            src_ref=predicted.at[pl.ds(peer * 2, 2)],
            dst_ref=back.at[pl.ds(me * 2, 2)],
            send_sem=b_out.at[peer],
            recv_sem=b_in.at[me],
            device_id={"tile": peer},
            device_id_type=MESH,
        )

    def send(step, carry):
        home((me + step) % TILES).start()
        return carry

    for k in range(1, CHAN):
        across(k).start()
    lax.fori_loop(1, TILES, send, 0)
    own = pltpu.make_async_copy(
        predicted.at[pl.ds(me * 2, 2)], back.at[pl.ds(me * 2, 2)], here.at[0]
    )
    own.start()
    total = summed[:, rows_of(chan), :]
    for k in range(1, CHAN):
        across(k).wait()
        total = total + parts[k - 1]
    combined[...] = total
    own.wait()

    def finish(step, carry):
        peer = (me + step) % TILES
        pltpu.make_async_copy(
            back.at[pl.ds(peer * 2, 2)], back.at[pl.ds(peer * 2, 2)], b_in.at[peer]
        ).wait()
        home(peer).wait_send()
        return carry

    lax.fori_loop(1, TILES, finish, 0)
    lower = lax.broadcasted_iota(jnp.int32, (16, 128), 0) < 8
    for b in range(16):
        word = info[b]
        alive = ((word >> 9) & 1) == 1
        flip = (1 - 2 * ((word >> 8) & 1)).astype(jnp.float32)
        value = back[word & 127].astype(jnp.float32)
        value = jnp.where(lower, value, value * flip)
        value = jnp.where(alive, value, jnp.float32(0.0))
        residual[b] = (vis[b].astype(jnp.float32) - value).astype(jnp.bfloat16)


def send_back(info, predicted, vis, summed):
    return pl.pallas_call(
        back_kernel,
        out_shape=(
            jax.ShapeDtypeStruct((16, 16, 128), jnp.bfloat16),
            jax.ShapeDtypeStruct((2, TS // CHAN, TS), jnp.float32),
        ),
        in_specs=[SMEM, VMEM, VMEM, VMEM],
        out_specs=(VMEM, VMEM),
        scratch_shapes=[
            pltpu.VMEM((SLOTS, 16, 128), jnp.bfloat16),
            pltpu.VMEM((CHAN - 1, 2, TS // CHAN, TS), jnp.float32),
            pltpu.SemaphoreType.DMA((TILES,)),
            pltpu.SemaphoreType.DMA((TILES,)),
            pltpu.SemaphoreType.DMA((CHAN - 1,)),
            pltpu.SemaphoreType.DMA((CHAN - 1,)),
            pltpu.SemaphoreType.DMA((1,)),
        ],
        compiler_params=pltpu.CompilerParams(
            collective_id=2, has_side_effects=True, vmem_limit_bytes=LIMIT
        ),
        name="send_back",
    )(info, predicted, vis, summed)


def per_device(visibility, imaging_weight, position, anchor, destination, block_count, kernel):
    vis = visibility.reshape(16, 16, 128)
    weight = imaging_weight.reshape(16, 8, 128)
    pos = position.reshape(16, 8, 128)
    rounded = lax.reduce_precision(kernel, 8, 7).T
    table = jnp.concatenate([rounded, rounded[::-1], jnp.zeros((TAPS, 64), jnp.float32)], axis=1)
    scaled, packed, info = sort_blocks(
        destination, block_count, anchor.reshape(32), vis, weight, pos
    )
    scaled, packed = route(scaled, packed)
    meta = packed.reshape(TILES, 2, 4, 128)[:, :, 0, 0].reshape(SLOTS)
    grid = grid_blocks(meta, scaled, packed, table)
    whole, summed = join_grids(grid)
    predicted = degrid_blocks(meta, packed, table, whole)
    residual, combined = send_back(info, predicted, vis, summed)
    upper = lax.axis_index("tile") >= TILES // 2
    sign = jnp.array([1.0, -1.0], jnp.float32).reshape(2, 1, 1)
    combined = jnp.where(upper, combined[:, ::-1, ::-1] * sign, combined)
    return combined, residual.reshape(visibility.shape)


def solution(mesh):
    placed = (
        P("tile", None, "chan", None),
        P("tile", "chan", None),
        P("tile", None, None),
        P("tile", None),
        P("tile"),
        P("tile"),
        P(),
    )
    return jax.shard_map(
        per_device,
        mesh=mesh,
        in_specs=placed,
        out_specs=(P(None, ("tile", "chan"), None), P("tile", None, "chan", None)),
        check_vma=False,
    )
```

time: 2340 us -> 123 us (0.05); the launches traced: 2300 us -> 123 us
  starting transfers between devices: 1880 us -> 0 us
  loops' own time: 120 us -> 0 us
  Pallas kernels: 0 us -> 109 us
  waiting for transfers between devices: 108 us -> 0 us
  local copies, waits for them, and re-layouts: 94.9 us -> 11.3 us
  other arithmetic: 65.7 us -> 1.52 us
    all_to_all x6 -> x0, starting transfers between devices: 1870 us -> none  [the longest x1 1830 us: per_device(): lax.all_to_all(slot_results, 'tile', split_axis=0, concat_axis=0, tiled=T...]
    another operation x2 -> x0, loops' own time: 120 us -> none  [the longest x1 60.6 us: per_device(): tile_grid = lax.fori_loop(jnp.int32(0), own_turns, grid_turn, tile_grid)]
    pallas_call x0 -> x6, Pallas kernels: none -> 109 us  [the longest x1 36.2 us: send_back(): pl.pallas_call(back_kernel, out_shape=(jax.ShapeDtypeStruct((16, 16, 128)...]
    dynamic_update_slice x16 -> x0, local copies, waits for them, and re-layouts: 49 us -> none  [grid_items(): lax.dynamic_update_slice(tile_grid, current + patches[item], start_at)]
    unnamed x2 -> x0, waiting for transfers between devices: 48.2 us -> none
    all_to_all x6 -> x0, waiting for transfers between devices: 47 us -> none  [the longest x1 14.3 us: per_device(): lax.all_to_all(send_positions, 'tile', split_axis=0, concat_axis=0, tiled...]
    convert_element_type x8 -> x0, other arithmetic: 24.6 us -> none  [the longest x1 9.85 us: per_device(): send_live = (filled & is_live[source]).astype(jnp.int32)]
  transfers between devices with their start and end apart: 8 -> 0, of which waited for: 7 -> 0; matrix products, arithmetic and copies ran while one was open for 1% -> 0% of each run, Pallas kernels for 0% -> 0%
where the time goes in v1:
time: 123 us
  Pallas kernels  109 us (89%)
  local copies, waits for them, and re-layouts  11.3 us (9%)
  other arithmetic  1.52 us (1%)
  between operations  1.39 us (1%)
    pallas_call x1, Pallas kernels, send_back(): pl.pallas_call(back_kernel, out_shape=(jax.ShapeDtypeStruct((16, 16, 128)...  36.2 us
    pallas_call x1, Pallas kernels, route(): pl.pallas_call(route_kernel, out_shape=(jax.ShapeDtypeStruct(scaled.shape...  32.8 us
    pallas_call x1, Pallas kernels, join_grids(): pl.pallas_call(join_kernel, out_shape=(jax.ShapeDtypeStruct((2, 4, TS, TS...  18.6 us
    pallas_call x1, Pallas kernels, degrid_blocks(): pl.pallas_call(degrid_kernel, out_shape=jax.ShapeDtypeStruct((SLOTS, 16,...  9.53 us
    pallas_call x1, Pallas kernels, grid_blocks(): pl.pallas_call(grid_kernel, out_shape=jax.ShapeDtypeStruct((2, 4, TS, TS)...  9.37 us
    unnamed x11, local copies, waits for them, and re-layouts  2.76 us

profile of v1, /device:TPU:1, one launch (start us, length us, event | category | flops | bytes accessed | tf_op | source)
XLA Modules:
  0.0 123.0 jit_solution(16226506436873812464)
XLA Ops:
  1.3 0.8 copy.12
  2.0 0.7 reshape.24.anchor
  2.7 1.5 %reshape.25.vis = bf16[16,16,128]{2,1,0:T(8,128)(2,1)} reshape(bf16[16,2,2,512]{3,2,1,0:T(2,128)(2,1)} %param.8) | data formatting | bytes 131072 | tf_op jit(solution)/shard_map/reshape | solution.py:491
  4.2 1.4 %reshape.26.weight = bf16[16,8,128]{2,1,0:T(8,128)(2,1)} reshape(bf16[16,2,512]{2,1,0:T(2,128)(2,1)} %param.9) | data formatting | bytes 65536 | tf_op jit(solution)/shard_map/reshape | solution.py:492
  5.6 1.5 %reshape.27.pos = s32[16,8,128]{2,1,0:T(8,128)} reshape(s32[16,2,512]{2,1,0:T(2,128)} %param.10) | data formatting | bytes 131072 | tf_op jit(solution)/shard_map/reshape | solution.py:493
  7.1 2.3 %sort_blocks.1 = (bf16[128,16,128]{2,1,0:T(8,128)(2,1)}, s32[64,8,128]{2,1,0:T(8,128)}, s32[16]{0:T(128)}) custom-call(s32[16]{0:T(128)} %dest.1, s32[1]{0:T(128)S(6)} %copy.15.count, s32[32]{0:T(128)} %reshape.24.anchor, bf16[16,16,128]{2,1,0:T(8,128)(2,1)} %reshape.25.vis, bf16[16,8,128]{2,1,0:T(8,128)(2,1)} %reshape.26.weight, s32[16,8,128]{2,1,0:T(8,128)} %reshape.27.pos), custom_call_target="tpu_custom_call" | custom-call | tf_op jit(solution)/shard_map/sort_blocks/pallas_call | solution.py:70
  9.4 0.0 copy-start.1
  9.4 1.0 copy-done.1
  10.4 0.0 copy-start.2
  10.4 0.9 copy-done.2
  11.4 32.8 %route.1 = (bf16[128,16,128]{2,1,0:T(8,128)(2,1)S(1)}, s32[64,8,128]{2,1,0:T(8,128)S(1)}) custom-call(bf16[128,16,128]{2,1,0:T(8,128)(2,1)S(1)} %copy-done.1, s32[64,8,128]{2,1,0:T(8,128)S(1)} %copy-done.2), custom_call_target="tpu_custom_call" | custom-call | tf_op jit(solution)/shard_map/route/pallas_call | solution.py:155
  44.2 2.3 %slice_reduce_fusion = s32[64,2]{1,0:T(8,128)S(1)} fusion(s32[64,2,4,128]{3,2,1,0:T(4,128)S(1)} %bitcast.3), kind=kLoop, calls=%fused_computation.1 | loop fusion | bytes 1024 | tf_op jit(solution)/shard_map/slice | solution.py:500
  46.5 0.1 reshape_squeeze.3.meta
  46.7 0.7 reduce-precision_bitcast_fusion
  47.4 0.1 pad.2.clone
  47.5 0.1 maximum_maximum_fusion.table
  47.6 9.4 %grid_blocks.1.grid = f32[2,4,256,256]{3,2,1,0:T(8,128)S(1)} custom-call(s32[128]{0:T(128)S(1)} %reshape_squeeze.3.meta, bf16[128,16,128]{2,1,0:T(8,128)(2,1)S(1)} %get-tuple-element.15.scaled, s32[64,8,128]{2,1,0:T(8,128)S(1)} %get-tuple-element.14.packed, f32[16,128]{1,0:T(8,128)S(1)} %maximum_maximum_fusion.table), custom_call_target="tpu_custom_call" | custom-call | tf_op jit(solution)/shard_map/grid_blocks/pallas_call | solution.py:263
  56.9 0.0 copy-start
  57.0 0.0 copy-start.3
  57.0 18.6 %join_grids.1 = (bf16[2,4,256,256]{3,2,1,0:T(8,128)(2,1)S(1)}, f32[2,256,256]{2,1,0:T(8,128)S(1)}) custom-call(f32[2,4,256,256]{3,2,1,0:T(8,128)S(1)} %grid_blocks.1.grid), custom_call_target="tpu_custom_call" | custom-call | tf_op jit(solution)/shard_map/join_grids/pallas_call | solution.py:324
  75.6 0.0 copy-start.4
  75.6 9.5 %degrid_blocks.1.predicted = bf16[128,16,128]{2,1,0:T(8,128)(2,1)S(1)} custom-call(s32[128]{0:T(128)S(1)} %reshape_squeeze.3.meta, s32[64,8,128]{2,1,0:T(8,128)S(1)} %get-tuple-element.14.packed, f32[16,128]{1,0:T(8,128)S(1)} %maximum_maximum_fusion.table, bf16[2,4,256,256]{3,2,1,0:T(8,128)(2,1)S(1)} %get-tuple-element.16.whole), custom_call_target="tpu_custom_call" | custom-call | tf_op jit(solution)/shard_map/degrid_blocks/pallas_call | solution.py:378
  85.1 0.0 copy-done
  85.1 0.0 copy-done.3
  85.1 36.2 %send_back.1 = (bf16[16,16,128]{2,1,0:T(8,128)(2,1)S(1)}, f32[2,64,256]{2,1,0:T(8,128)S(1)}) custom-call(s32[16]{0:T(128)S(1)} %copy-done.3, bf16[128,16,128]{2,1,0:T(8,128)(2,1)S(1)} %degrid_blocks.1.predicted, bf16[16,16,128]{2,1,0:T(8,128)(2,1)S(1)} %copy-done, f32[2,256,256]{2,1,0:T(8,128)S(1)} %get-tuple-element.17.summed), custom_call_target="tpu_custom_call" | custom-call | tf_op jit(solution)/shard_map/send_back/pallas_call | solution.py:466
  121.4 0.2 rev.7
  121.6 0.0 copy-done.4
  121.6 0.7 multiply_select_fusion
  122.3 0.7 reshape.29
  (2 shorter events, 0.0 us)
Async XLA Ops:
  9.4 1.0 copy-start.1
  10.4 0.9 copy-start.2
  56.9 28.2 %copy-start = (bf16[16,16,128]{2,1,0:T(8,128)(2,1)S(1)}, bf16[16,16,128]{2,1,0:T(8,128)(2,1)}, u32[]{:S(2)}) copy-start(bf16[16,16,128]{2,1,0:T(8,128)(2,1)} %reshape.25.vis) | copy-start | bytes 196612
  57.0 28.2 %copy-start.3 = (s32[16]{0:T(128)S(1)}, s32[16]{0:T(128)}, u32[]{:S(2)}) copy-start(s32[16]{0:T(128)} %get-tuple-element.11.info) | copy-start | bytes 196
  75.6 46.0 %copy-start.4 = (f32[2]{0:T(128)S(1)}, f32[2]{0:T(128)}, u32[]{:S(2)}) copy-start(f32[2]{0:T(128)} %constant.12.clone) | copy-start | bytes 28

commit v2 on v1

--- a/solution.py
+++ b/solution.py
@@ -7,6 +7,7 @@
 from jax.experimental.pallas import tpu as pltpu
 from jax.sharding import PartitionSpec as P
 
+BLOCK = 512
 TAPS = 16
 OS = 32
 SUB = 128
@@ -20,17 +21,56 @@
 
 VMEM = pl.BlockSpec(memory_space=pltpu.VMEM)
 SMEM = pl.BlockSpec(memory_space=pltpu.SMEM)
+HBM = pl.BlockSpec(memory_space=pltpu.HBM)
 MESH = pl.DeviceIdType.MESH
 
 
-def sort_kernel(dest, count, anchor, vis, weight, pos, scaled, packed, info, used):
+def sort_kernel(
+    dest,
+    count,
+    anchor,
+    far_vis,
+    far_weight,
+    far_pos,
+    kernel,
+    scaled,
+    packed,
+    info,
+    table,
+    used,
+    vis,
+    weight,
+    pos,
+    sems,
+):
+    fetches = [
+        pltpu.make_async_copy(source, target, sems.at[k])
+        for k, (source, target) in enumerate(((far_vis, vis), (far_weight, weight), (far_pos, pos)))
+    ]
+    for fetch in fetches:
+        fetch.start()
     me = lax.axis_index("tile")
     turn = me + (me >> 2) + (me >> 4)
     scaled[...] = jnp.zeros(scaled.shape, scaled.dtype)
     packed[...] = jnp.zeros(packed.shape, packed.dtype)
     for quad in range(TILES // 4):
         used[quad] = 0
-    half = lax.broadcasted_iota(jnp.int32, (8, 128), 0) // GROUPS
+
+    def ones_where(mask):
+        return jnp.where(mask, jnp.float32(1.0), jnp.float32(0.0)).astype(jnp.bfloat16)
+
+    def iota(shape, axis):
+        return lax.broadcasted_iota(jnp.int32, shape, axis)
+
+    values = kernel[...].astype(jnp.bfloat16)
+    swap = ones_where(iota((TAPS, TAPS), 0) + iota((TAPS, TAPS), 1) == TAPS - 1)
+    turned = jnp.dot(swap, values, preferred_element_type=jnp.float32).astype(jnp.bfloat16)
+    spread = iota((OS, 128), 1) - iota((OS, 128), 0)
+    table[...] = jnp.dot(
+        values, ones_where(spread == 0), preferred_element_type=jnp.float32
+    ) + jnp.dot(turned, ones_where(spread == OS), preferred_element_type=jnp.float32)
+    for fetch in fetches:
+        fetch.wait()
     for b in range(16):
         alive = (b < count[0]).astype(jnp.int32)
         tile = dest[b]
@@ -42,8 +82,8 @@
         which = rank >> 2
         mirror = tile >> 5
         flip = 1 - 2 * mirror
-        top = mirror * (TS - SUB) + flip * anchor[2 * b]
-        left = mirror * (TS - SUB) + flip * anchor[2 * b + 1]
+        top = mirror * (TS - SUB) + flip * anchor[0, b]
+        left = mirror * (TS - SUB) + flip * anchor[1, b]
         base = jnp.minimum(top >> 4, 7)
         info[b] = (device * 2 + which) | (mirror << 8) | (alive << 9)
         meta = (alive << 26) | (base << 27) | (mirror << 30) | ((tile & 1) << 31)
@@ -53,32 +93,37 @@
             place = pos[b]
             cell = mirror * (SUB - TAPS) + flip * (place >> 5)
             offset = place & (OS - 1)
-            row = (cell[:4] + (top - base * 16)) * OS + offset[:4]
-            column = (cell[4:] + left) * OS + offset[4:]
-            word = row | (column << 13) | meta
-            both = jnp.concatenate([word, word], axis=0)
-            packed[device] = jnp.where(half == which, both, packed[device])
-            values = vis[b].astype(jnp.float32)
+            row = (cell[0:1] + (top - base * 16)) * OS + offset[0:1]
+            column = (cell[1:2] + left) * OS + offset[1:2]
+            packed[device, pl.ds(which, 1), :] = row | (column << 13) | meta
             factor = weight[b].astype(jnp.float32)
             sign = flip.astype(jnp.float32)
-            scaled[device * 2 + which] = jnp.concatenate(
-                [values[:8] * factor, values[8:] * factor * sign], axis=0
-            ).astype(jnp.bfloat16)
-
-
-def sort_blocks(dest, count, anchor, vis, weight, pos):
+            slot = device * 2 + which
+            scaled[slot, 0] = (vis[b, 0].astype(jnp.float32) * factor).astype(jnp.bfloat16)
+            scaled[slot, 1] = (vis[b, 1].astype(jnp.float32) * (factor * sign)).astype(jnp.bfloat16)
+
+
+def sort_blocks(dest, count, anchor, vis, weight, pos, kernel):
     return pl.pallas_call(
         sort_kernel,
         out_shape=(
-            jax.ShapeDtypeStruct((SLOTS, 16, 128), jnp.bfloat16),
-            jax.ShapeDtypeStruct((TILES, 8, 128), jnp.int32),
+            jax.ShapeDtypeStruct((SLOTS, 2, 2, BLOCK), jnp.bfloat16),
+            jax.ShapeDtypeStruct((TILES, 2, BLOCK), jnp.int32),
             jax.ShapeDtypeStruct((16,), jnp.int32),
-        ),
-        in_specs=[SMEM, SMEM, SMEM, VMEM, VMEM, VMEM],
-        out_specs=(VMEM, VMEM, SMEM),
-        scratch_shapes=[pltpu.SMEM((TILES // 4,), jnp.int32)],
+            jax.ShapeDtypeStruct((TAPS, 128), jnp.float32),
+        ),
+        in_specs=[SMEM, SMEM, SMEM, HBM, HBM, HBM, VMEM],
+        out_specs=(VMEM, VMEM, SMEM, VMEM),
+        scratch_shapes=[
+            pltpu.SMEM((TILES // 4,), jnp.int32),
+            pltpu.VMEM(vis.shape, vis.dtype),
+            pltpu.VMEM(weight.shape, weight.dtype),
+            pltpu.VMEM(pos.shape, pos.dtype),
+            pltpu.SemaphoreType.DMA((3,)),
+        ],
+        compiler_params=pltpu.CompilerParams(vmem_limit_bytes=LIMIT),
         name="sort_blocks",
-    )(dest, count, anchor, vis, weight, pos)
+    )(dest, count, anchor, vis, weight, pos, kernel)
 
 
 def greet_tiles(me):
@@ -168,23 +213,28 @@
     )(scaled, packed)
 
 
-def gather_live(meta, order):
-    def look(slot, count):
-        order[count] = slot
-        return count + ((meta[slot] >> 26) & 1)
-
-    count = lax.fori_loop(0, SLOTS, look, jnp.int32(0))
-    return count
-
-
-def tap_rows(table, cell, column, pieces):
+def live_turns(count, one):
+    def many(start, width):
+        def step(turn, carry):
+            for k in range(width):
+                at = start + turn * width + k
+                one(jnp.where(at < count, at, 0), at < count)
+            return carry
+
+        return step
+
+    eights = count >> 3
+    lax.fori_loop(0, eights, many(0, 8), 0)
+    lax.fori_loop(0, (count - eights * 8 + 1) >> 1, many(eights * 8, 2), 0)
+
+
+def tap_tiles(table, cell, column, pieces):
     cell = jnp.broadcast_to(cell, (8, 128))
     column = jnp.broadcast_to(column, (8, 128))
     low = jnp.take_along_axis(table[:8], column, axis=1, mode="promise_in_bounds")
     high = jnp.take_along_axis(table[8:], column, axis=1, mode="promise_in_bounds")
     sub = lax.broadcasted_iota(jnp.int32, (8, 128), 0)
     part = cell & 7
-    whole = cell >> 3
     turn = (sub - part) & 7
     low = jnp.take_along_axis(low, turn, axis=0, mode="promise_in_bounds")
     high = jnp.take_along_axis(high, turn, axis=0, mode="promise_in_bounds")
@@ -193,82 +243,103 @@
     first = jnp.where(after, low, zero)
     second = jnp.where(after, high, low)
     third = jnp.where(after, zero, high)
-    at = [whole == m for m in range(pieces)]
-    rows = []
+    late = (cell & 8) == 8
+
+    def both(upper, lower):
+        return jnp.concatenate([upper, lower], axis=0).astype(jnp.bfloat16)
+
+    begin = both(jnp.where(late, zero, first), jnp.where(late, first, second))
+    end = both(jnp.where(late, second, third), jnp.where(late, third, zero))
+    whole = (cell >> 4).astype(jnp.float32)
+    whole = both(whole, whole)
+    blank = jnp.zeros((16, 128), jnp.bfloat16)
+    at = [whole == jnp.bfloat16(m) for m in range(pieces)]
+    tiles = []
     for m in range(pieces):
-        value = zero
-        if m >= 2:
-            value = jnp.where(at[m - 2], third, value)
-        if m >= 1:
-            value = jnp.where(at[m - 1], second, value)
-        rows.append(jnp.where(at[m], first, value))
-    return jnp.concatenate(rows, axis=0)
+        value = jnp.where(at[m - 1], end, blank) if m else blank
+        tiles.append(jnp.where(at[m], begin, value))
+    return tiles
 
 
 def slot_taps(packed, table, slot, word):
     both = packed[slot >> 1]
-    mine = jnp.where((slot & 1) == 1, both[4:], both[:4])
+    mine = jnp.where((slot & 1) == 1, both[1:2], both[0:1])
     shift = OS * ((word >> 30) & 1)
     row_cell = (mine >> 5) & 255
     row_column = (mine & (OS - 1)) + shift
     col_cell = (mine >> 18) & 255
     col_column = ((mine >> 13) & (OS - 1)) + shift
-    rows = [
-        tap_rows(table, row_cell[g : g + 1], row_column[g : g + 1], ROWS // 8)
-        for g in range(GROUPS)
-    ]
+    lanes = [slice(g * 128, (g + 1) * 128) for g in range(GROUPS)]
+    rows = [tap_tiles(table, row_cell[:, k], row_column[:, k], ROWS // 16) for k in lanes]
     cols = [
-        tap_rows(table, col_cell[g : g + 1], col_column[g : g + 1], TS // 8).astype(jnp.bfloat16)
-        for g in range(GROUPS)
+        jnp.concatenate(tap_tiles(table, col_cell[:, k], col_column[:, k], TS // 16), axis=0)
+        for k in lanes
     ]
     return rows, jnp.concatenate(cols, axis=1)
 
 
-def grid_kernel(meta, scaled, packed, table, grid, order):
-    count = gather_live(meta, order)
+def grid_kernel(scaled, packed, table, grid, live, words, line, heads, sem):
+    flags = jnp.concatenate([packed[:, 0, 0:128], packed[:, 1, 0:128]], axis=0)
+    line[...] = jnp.broadcast_to(flags.T[0:1], (8, 128))
+    fetch = pltpu.make_async_copy(line, heads, sem)
+    fetch.start()
     grid[...] = jnp.zeros(grid.shape, grid.dtype)
     taps = table[...]
-
-    def one(slot, keep):
-        word = meta[slot]
+    fetch.wait()
+
+    def look(device, count):
+        for which in range(2):
+            word = heads[0, which * TILES + device]
+            live[count] = device * 2 + which
+            words[count] = word
+            count = count + ((word >> 26) & 1)
+        return count
+
+    count = lax.fori_loop(0, TILES, look, jnp.int32(0), unroll=4)
+    live[SLOTS] = count
+
+    def one(k, alive):
+        slot, word = live[k], words[k]
         rows, cols = slot_taps(packed, taps, slot, word)
-        values = scaled[slot].astype(jnp.float32) * keep
+        keep = alive.astype(jnp.float32)
         planes = []
-        for plane in range(4):
-            parts = [
-                (rows[g] * values[plane * GROUPS + g : plane * GROUPS + g + 1]).astype(jnp.bfloat16)
-                for g in range(GROUPS)
-            ]
-            planes.append(jnp.concatenate(parts, axis=1))
-        left = jnp.concatenate(planes, axis=0)
+        for part in range(2):
+            values = scaled[slot, part].astype(jnp.float32) * keep
+            for channel in range(2):
+                lanes = []
+                for g in range(GROUPS):
+                    value = values[channel : channel + 1, g * 128 : (g + 1) * 128]
+                    value = jnp.broadcast_to(value, (16, 128)).astype(jnp.bfloat16)
+                    lanes.append(jnp.concatenate([tile * value for tile in rows[g]], axis=0))
+                planes.append(jnp.concatenate(lanes, axis=1))
         product = lax.dot_general(
-            left, cols, (((1,), (1,)), ((), ())), preferred_element_type=jnp.float32
-        )
-        which = (word >> 31) & 1
+            jnp.concatenate(planes, axis=0),
+            cols,
+            (((1,), (1,)), ((), ())),
+            preferred_element_type=jnp.float32,
+        )
+        pair = (word >> 31) & 1
         start = pl.multiple_of(((word >> 27) & 7) * 16, 16)
         for plane in range(4):
-            grid[which, plane, pl.ds(start, ROWS), :] += product[plane * ROWS : (plane + 1) * ROWS]
-
-    def step(turn, carry):
-        one(order[2 * turn], jnp.float32(1.0))
-        later = 2 * turn + 1
-        extra = later < count
-        one(order[jnp.where(extra, later, 0)], extra.astype(jnp.float32))
-        return carry
-
-    lax.fori_loop(0, (count + 1) >> 1, step, 0)
-
-
-def grid_blocks(meta, scaled, packed, table):
+            grid[pair, plane, pl.ds(start, ROWS), :] += product[plane * ROWS : (plane + 1) * ROWS]
+
+    live_turns(count, one)
+
+
+def grid_blocks(scaled, packed, table):
     return pl.pallas_call(
         grid_kernel,
-        out_shape=jax.ShapeDtypeStruct((2, 4, TS, TS), jnp.float32),
-        in_specs=[SMEM, VMEM, VMEM, VMEM],
-        out_specs=VMEM,
-        scratch_shapes=[pltpu.SMEM((SLOTS + 8,), jnp.int32)],
+        out_shape=(
+            jax.ShapeDtypeStruct((2, 4, TS, TS), jnp.float32),
+            jax.ShapeDtypeStruct((SLOTS + 8,), jnp.int32),
+            jax.ShapeDtypeStruct((SLOTS + 8,), jnp.int32),
+        ),
+        in_specs=[VMEM, VMEM, VMEM],
+        out_specs=(VMEM, SMEM, SMEM),
+        scratch_shapes=[pltpu.VMEM((8, 128), jnp.int32), pltpu.SMEM((8, 128), jnp.int32), pltpu.SemaphoreType.DMA],
         compiler_params=pltpu.CompilerParams(vmem_limit_bytes=LIMIT),
         name="grid_blocks",
-    )(meta, scaled, packed, table)
+    )(scaled, packed, table)
 
 
 def join_kernel(grid, whole, summed, half, got_half, total, mine, got_mine, send, recv):
@@ -345,45 +416,68 @@
     )(grid)
 
 
-def degrid_kernel(meta, packed, table, whole, predicted, order):
-    count = gather_live(meta, order)
+def turn_over(value):
+    sub = lax.broadcasted_iota(jnp.int32, (8, 128), 0)
+    lane = lax.broadcasted_iota(jnp.int32, (8, 128), 1)
+
+    def reverse(tile):
+        tile = jnp.take_along_axis(tile, 127 - lane, axis=1, mode="promise_in_bounds")
+        return jnp.take_along_axis(tile, 7 - sub, axis=0, mode="promise_in_bounds")
+
+    rows = []
+    for m in reversed(range(TS // 8)):
+        tiles = [reverse(value[m * 8 : m * 8 + 8, k * 128 : k * 128 + 128]) for k in (1, 0)]
+        rows.append(jnp.concatenate(tiles, axis=1))
+    return jnp.concatenate(rows, axis=0)
+
+
+def degrid_kernel(live, words, packed, table, whole, summed, predicted, framed):
+    upper = lax.axis_index("tile") // (TILES // 2)
     taps = table[...]
 
-    def one(slot):
-        word = meta[slot]
+    @pl.when(upper == 1)
+    def _():
+        framed[0] = turn_over(summed[0])
+        framed[1] = -turn_over(summed[1])
+
+    @pl.when(upper == 0)
+    def _():
+        framed[...] = summed[...]
+
+    def one(k, alive):
+        slot, word = live[k], words[k]
         rows, cols = slot_taps(packed, taps, slot, word)
-        which = (word >> 31) & 1
+        rows = [jnp.concatenate(tiles, axis=0).astype(jnp.float32) for tiles in rows]
+        pair = (word >> 31) & 1
         start = pl.multiple_of(((word >> 27) & 7) * 16, 16)
-        results = []
-        for plane in range(4):
-            window = whole[which, plane, pl.ds(start, ROWS), :]
-            across = jnp.dot(window, cols, preferred_element_type=jnp.float32)
-            for g in range(GROUPS):
-                results.append(
+        scale = jnp.float32(1.0 / (TAPS * TAPS))
+        for part in range(2):
+            results = []
+            for channel in range(2):
+                window = whole[pair, part * 2 + channel, pl.ds(start, ROWS), :]
+                across = jnp.dot(window, cols, preferred_element_type=jnp.float32)
+                sums = [
                     jnp.sum(rows[g] * across[:, g * 128 : (g + 1) * 128], axis=0, keepdims=True)
-                )
-        scale = jnp.float32(1.0 / (TAPS * TAPS))
-        predicted[slot] = (jnp.concatenate(results, axis=0) * scale).astype(jnp.bfloat16)
-
-    def step(turn, carry):
-        one(order[2 * turn])
-        later = 2 * turn + 1
-        one(order[jnp.where(later < count, later, 0)])
-        return carry
-
-    lax.fori_loop(0, (count + 1) >> 1, step, 0)
-
-
-def degrid_blocks(meta, packed, table, whole):
+                    for g in range(GROUPS)
+                ]
+                results.append(jnp.concatenate(sums, axis=1))
+            predicted[slot, part] = (jnp.concatenate(results, axis=0) * scale).astype(jnp.bfloat16)
+
+    live_turns(live[SLOTS], one)
+
+
+def degrid_blocks(live, words, packed, table, whole, summed):
     return pl.pallas_call(
         degrid_kernel,
-        out_shape=jax.ShapeDtypeStruct((SLOTS, 16, 128), jnp.bfloat16),
-        in_specs=[SMEM, VMEM, VMEM, VMEM],
-        out_specs=VMEM,
-        scratch_shapes=[pltpu.SMEM((SLOTS + 8,), jnp.int32)],
+        out_shape=(
+            jax.ShapeDtypeStruct((SLOTS, 2, 2, BLOCK), jnp.bfloat16),
+            jax.ShapeDtypeStruct((2, TS, TS), jnp.float32),
+        ),
+        in_specs=[SMEM, SMEM, VMEM, VMEM, VMEM, VMEM],
+        out_specs=(VMEM, VMEM),
         compiler_params=pltpu.CompilerParams(vmem_limit_bytes=LIMIT),
         name="degrid_blocks",
-    )(meta, packed, table, whole)
+    )(live, words, packed, table, whole, summed)
 
 
 def back_kernel(
@@ -391,7 +485,6 @@
 ):
     me = lax.axis_index("tile")
     chan = lax.axis_index("chan")
-    upper = me // (TILES // 2)
     barrier = greet_tiles(me)
     for k in range(1, CHAN):
         pl.semaphore_signal(
@@ -400,8 +493,7 @@
     pl.semaphore_wait(barrier, TILES - 1 + CHAN - 1)
 
     def rows_of(group):
-        place = group + upper * (CHAN - 1 - 2 * group)
-        return pl.ds(pl.multiple_of(place * (TS // CHAN), TS // CHAN), TS // CHAN)
+        return pl.ds(pl.multiple_of(group * (TS // CHAN), TS // CHAN), TS // CHAN)
 
     def across(k):
         group = (chan + k) % CHAN
@@ -451,28 +543,31 @@
         return carry
 
     lax.fori_loop(1, TILES, finish, 0)
-    lower = lax.broadcasted_iota(jnp.int32, (16, 128), 0) < 8
-    for b in range(16):
-        word = info[b]
-        alive = ((word >> 9) & 1) == 1
-        flip = (1 - 2 * ((word >> 8) & 1)).astype(jnp.float32)
-        value = back[word & 127].astype(jnp.float32)
-        value = jnp.where(lower, value, value * flip)
-        value = jnp.where(alive, value, jnp.float32(0.0))
-        residual[b] = (vis[b].astype(jnp.float32) - value).astype(jnp.bfloat16)
+    for first in range(0, 16, 4):
+        results = []
+        for b in range(first, first + 4):
+            word = info[b]
+            keep = ((word >> 9) & 1).astype(jnp.float32)
+            flip = (1 - 2 * ((word >> 8) & 1)).astype(jnp.float32)
+            for part in range(2):
+                value = back[word & 127, part].astype(jnp.float32)
+                value = jnp.where(keep > 0.5, value * flip if part else value, jnp.float32(0.0))
+                results.append((vis[b, part].astype(jnp.float32) - value).astype(jnp.bfloat16))
+        for k, result in enumerate(results):
+            residual[first + k // 2, k % 2] = result
 
 
 def send_back(info, predicted, vis, summed):
     return pl.pallas_call(
         back_kernel,
         out_shape=(
-            jax.ShapeDtypeStruct((16, 16, 128), jnp.bfloat16),
+            jax.ShapeDtypeStruct(vis.shape, vis.dtype),
             jax.ShapeDtypeStruct((2, TS // CHAN, TS), jnp.float32),
         ),
         in_specs=[SMEM, VMEM, VMEM, VMEM],
         out_specs=(VMEM, VMEM),
         scratch_shapes=[
-            pltpu.VMEM((SLOTS, 16, 128), jnp.bfloat16),
+            pltpu.VMEM((SLOTS, 2, 2, BLOCK), jnp.bfloat16),
             pltpu.VMEM((CHAN - 1, 2, TS // CHAN, TS), jnp.float32),
             pltpu.SemaphoreType.DMA((TILES,)),
             pltpu.SemaphoreType.DMA((TILES,)),
@@ -488,24 +583,15 @@
 
 
 def per_device(visibility, imaging_weight, position, anchor, destination, block_count, kernel):
-    vis = visibility.reshape(16, 16, 128)
-    weight = imaging_weight.reshape(16, 8, 128)
-    pos = position.reshape(16, 8, 128)
-    rounded = lax.reduce_precision(kernel, 8, 7).T
-    table = jnp.concatenate([rounded, rounded[::-1], jnp.zeros((TAPS, 64), jnp.float32)], axis=1)
-    scaled, packed, info = sort_blocks(
-        destination, block_count, anchor.reshape(32), vis, weight, pos
+    scaled, packed, info, table = sort_blocks(
+        destination, block_count, anchor.T, visibility, imaging_weight, position, kernel.T
     )
     scaled, packed = route(scaled, packed)
-    meta = packed.reshape(TILES, 2, 4, 128)[:, :, 0, 0].reshape(SLOTS)
-    grid = grid_blocks(meta, scaled, packed, table)
+    grid, live, words = grid_blocks(scaled, packed, table)
     whole, summed = join_grids(grid)
-    predicted = degrid_blocks(meta, packed, table, whole)
-    residual, combined = send_back(info, predicted, vis, summed)
-    upper = lax.axis_index("tile") >= TILES // 2
-    sign = jnp.array([1.0, -1.0], jnp.float32).reshape(2, 1, 1)
-    combined = jnp.where(upper, combined[:, ::-1, ::-1] * sign, combined)
-    return combined, residual.reshape(visibility.shape)
+    predicted, framed = degrid_blocks(live, words, packed, table, whole, summed)
+    residual, combined = send_back(info, predicted, visibility, framed)
+    return combined, residual
 
 
 def solution(mesh):

time: 123 us -> 106 us (0.86)
  Pallas kernels: 109 us -> 98.2 us
  local copies, waits for them, and re-layouts: 11.3 us -> 5.75 us
  other arithmetic: 1.52 us -> 0 us
    pallas_call x4, Pallas kernels: 57.4 us -> 46.9 us  [the longest x1 38.9 us: send_back(): pl.pallas_call(back_kernel, out_shape=(jax.ShapeDtypeStruct(vis.shape, vi...]
    reshape x5 -> x0, local copies, waits for them, and re-layouts: 5.75 us -> none  [the longest x1 1.52 us: per_device(): pos = position.reshape(16, 8, 128)]
    unnamed x11 -> x16, local copies, waits for them, and re-layouts: 2.76 us -> 5.75 us
    slice x1 -> x0, local copies, waits for them, and re-layouts: 2.34 us -> none  [per_device(): meta = packed.reshape(TILES, 2, 4, 128)[:, :, 0, 0].reshape(SLOTS)]
where the time goes in v2:
time: 106 us; the launch traced here: 105 us
  Pallas kernels  98.2 us (93%)
  local copies, waits for them, and re-layouts  5.75 us (5%)
  between operations  1.36 us (1%)
    pallas_call x1, Pallas kernels, send_back(): pl.pallas_call(back_kernel, out_shape=(jax.ShapeDtypeStruct(vis.shape, vi...  38.9 us
    pallas_call x1, Pallas kernels, route(): pl.pallas_call(route_kernel, out_shape=(jax.ShapeDtypeStruct(scaled.shape...  33.2 us
    pallas_call x1, Pallas kernels, join_grids(): pl.pallas_call(join_kernel, out_shape=(jax.ShapeDtypeStruct((2, 4, TS, TS...  18.1 us
    unnamed x16, local copies, waits for them, and re-layouts  5.75 us
    pallas_call x1, Pallas kernels, grid_blocks(): pl.pallas_call(grid_kernel, out_shape=(jax.ShapeDtypeStruct((2, 4, TS, TS...  3.56 us
    pallas_call x1, Pallas kernels, degrid_blocks(): pl.pallas_call(degrid_kernel, out_shape=(jax.ShapeDtypeStruct((SLOTS, 2,...  2.4 us

profile of v2, /device:TPU:1, one launch (start us, length us, event | category | flops | bytes accessed | tf_op | source)
XLA Modules:
  0.0 105.3 jit_solution(14686422595653455168)
XLA Ops:
  1.3 0.0 copy-start
  1.3 0.8 copy-done
  2.1 0.0 copy-start.2
  2.1 0.8 copy-done.2
  3.0 0.0 copy-start.3
  3.0 0.8 copy-done.3
  3.7 0.0 copy-start.4
  3.7 0.7 copy-done.4
  4.4 0.0 copy-start.5
  4.4 0.7 copy-done.5
  5.1 0.0 copy-start.6
  5.1 0.7 copy-done.6
  5.8 2.0 %sort_blocks.1 = (bf16[128,2,2,512]{3,2,1,0:T(2,128)(2,1)S(1)}, s32[64,2,512]{2,1,0:T(2,128)S(1)}, s32[16]{0:T(128)S(1)}, f32[16,128]{1,0:T(8,128)S(1)}) custom-call(s32[16]{0:T(128)S(1)} %copy-done.6, s32[1]{0:T(128)S(6)} %copy.11.count, s32[2,16]{1,0:T(2,128)S(1)} %bitcast.3, bf16[16,2,2,512]{3,2,1,0:T(2,128)(2,1)S(1)} %copy-done, ...), custom_call_target="tpu_custom_call" | custom-call | tf_op jit(solution)/shard_map/sort_blocks/pallas_call | solution.py:107
  7.8 33.2 %route.1 = (bf16[128,2,2,512]{3,2,1,0:T(2,128)(2,1)S(1)}, s32[64,2,512]{2,1,0:T(2,128)S(1)}) custom-call(bf16[128,2,2,512]{3,2,1,0:T(2,128)(2,1)S(1)} %get-tuple-element.18.scaled, s32[64,2,512]{2,1,0:T(2,128)S(1)} %get-tuple-element.19.packed), custom_call_target="tpu_custom_call" | custom-call | tf_op jit(solution)/shard_map/route/pallas_call | solution.py:200
  41.0 3.6 %grid_blocks.1 = (f32[2,4,256,256]{3,2,1,0:T(8,128)S(1)}, s32[136]{0:T(256)S(1)}, s32[136]{0:T(256)S(1)}) custom-call(bf16[128,2,2,512]{3,2,1,0:T(2,128)(2,1)S(1)} %get-tuple-element.20.scaled, s32[64,2,512]{2,1,0:T(2,128)S(1)} %get-tuple-element.21.packed, f32[16,128]{1,0:T(8,128)S(1)} %get-tuple-element.22.table), custom_call_target="tpu_custom_call" | custom-call | tf_op jit(solution)/shard_map/grid_blocks/pallas_call | solution.py:330
  44.6 0.0 copy-start.1
  44.6 18.1 %join_grids.1 = (bf16[2,4,256,256]{3,2,1,0:T(8,128)(2,1)S(1)}, f32[2,256,256]{2,1,0:T(8,128)S(1)}) custom-call(f32[2,4,256,256]{3,2,1,0:T(8,128)S(1)} %get-tuple-element.25.grid), custom_call_target="tpu_custom_call" | custom-call | tf_op jit(solution)/shard_map/join_grids/pallas_call | solution.py:395
  62.7 2.4 %degrid_blocks.1 = (bf16[128,2,2,512]{3,2,1,0:T(2,128)(2,1)S(1)}, f32[2,256,256]{2,1,0:T(8,128)S(1)}) custom-call(s32[136]{0:T(256)S(1)} %get-tuple-element.23.live, s32[136]{0:T(256)S(1)} %get-tuple-element.24.words, s32[64,2,512]{2,1,0:T(2,128)S(1)} %get-tuple-element.21.packed, f32[16,128]{1,0:T(8,128)S(1)} %get-tuple-element.22.table, ...), custom_call_target="tpu_custom_call" | custom-call | tf_op jit(solution)/shard_map/degrid_blocks/pallas_call | solution.py:470
  65.1 0.0 copy-done.1
  65.1 38.9 %send_back.1 = (bf16[16,2,2,512]{3,2,1,0:T(2,128)(2,1)S(1)}, f32[2,64,256]{2,1,0:T(8,128)S(1)}) custom-call(s32[16]{0:T(128)S(1)} %get-tuple-element.17.info, bf16[128,2,2,512]{3,2,1,0:T(2,128)(2,1)S(1)} %get-tuple-element.28.predicted, bf16[16,2,2,512]{3,2,1,0:T(2,128)(2,1)S(1)} %copy-done.1, f32[2,256,256]{2,1,0:T(8,128)S(1)} %get-tuple-element.29.summed), custom_call_target="tpu_custom_call" | custom-call | tf_op jit(solution)/shard_map/send_back/pallas_call | solution.py:561
  104.1 0.7 copy.12
  104.7 0.6 copy.13
Async XLA Ops:
  1.3 0.8 copy-start
  2.1 0.8 copy-start.2
  3.0 0.8 copy-start.3
  3.7 0.7 copy-start.4
  4.4 0.7 copy-start.5
  5.1 0.7 copy-start.6
  44.6 20.5 %copy-start.1 = (bf16[16,2,2,512]{3,2,1,0:T(2,128)(2,1)S(1)}, bf16[16,2,2,512]{3,2,1,0:T(2,128)(2,1)}, u32[]{:S(2)}) copy-start(bf16[16,2,2,512]{3,2,1,0:T(2,128)(2,1)} %vis.1) | copy-start | bytes 196612

commit v3 on v2

--- a/solution.py
+++ b/solution.py
@@ -26,26 +26,38 @@
 
 
 def sort_kernel(
-    dest,
+    far_dest,
     count,
-    anchor,
+    far_anchor,
     far_vis,
     far_weight,
     far_pos,
-    kernel,
+    far_kernel,
     scaled,
     packed,
     info,
     table,
     used,
+    dest,
+    anchor,
     vis,
     weight,
     pos,
+    kernel,
     sems,
 ):
     fetches = [
         pltpu.make_async_copy(source, target, sems.at[k])
-        for k, (source, target) in enumerate(((far_vis, vis), (far_weight, weight), (far_pos, pos)))
+        for k, (source, target) in enumerate(
+            (
+                (far_dest, dest),
+                (far_anchor, anchor),
+                (far_vis, vis),
+                (far_weight, weight),
+                (far_pos, pos),
+                (far_kernel, kernel),
+            )
+        )
     ]
     for fetch in fetches:
         fetch.start()
@@ -62,6 +74,7 @@
     def iota(shape, axis):
         return lax.broadcasted_iota(jnp.int32, shape, axis)
 
+    fetches[5].wait()
     values = kernel[...].astype(jnp.bfloat16)
     swap = ones_where(iota((TAPS, TAPS), 0) + iota((TAPS, TAPS), 1) == TAPS - 1)
     turned = jnp.dot(swap, values, preferred_element_type=jnp.float32).astype(jnp.bfloat16)
@@ -69,7 +82,7 @@
     table[...] = jnp.dot(
         values, ones_where(spread == 0), preferred_element_type=jnp.float32
     ) + jnp.dot(turned, ones_where(spread == OS), preferred_element_type=jnp.float32)
-    for fetch in fetches:
+    for fetch in fetches[:5]:
         fetch.wait()
     for b in range(16):
         alive = (b < count[0]).astype(jnp.int32)
@@ -103,6 +116,10 @@
             scaled[slot, 1] = (vis[b, 1].astype(jnp.float32) * (factor * sign)).astype(jnp.bfloat16)
 
 
+def in_hbm(array):
+    return pltpu.with_memory_space_constraint(array, pltpu.HBM)
+
+
 def sort_blocks(dest, count, anchor, vis, weight, pos, kernel):
     return pl.pallas_call(
         sort_kernel,
@@ -112,18 +129,21 @@
             jax.ShapeDtypeStruct((16,), jnp.int32),
             jax.ShapeDtypeStruct((TAPS, 128), jnp.float32),
         ),
-        in_specs=[SMEM, SMEM, SMEM, HBM, HBM, HBM, VMEM],
+        in_specs=[HBM, SMEM, HBM, HBM, HBM, HBM, HBM],
         out_specs=(VMEM, VMEM, SMEM, VMEM),
         scratch_shapes=[
             pltpu.SMEM((TILES // 4,), jnp.int32),
+            pltpu.SMEM(dest.shape, dest.dtype),
+            pltpu.SMEM(anchor.shape, anchor.dtype),
             pltpu.VMEM(vis.shape, vis.dtype),
             pltpu.VMEM(weight.shape, weight.dtype),
             pltpu.VMEM(pos.shape, pos.dtype),
-            pltpu.SemaphoreType.DMA((3,)),
+            pltpu.VMEM(kernel.shape, kernel.dtype),
+            pltpu.SemaphoreType.DMA((6,)),
         ],
         compiler_params=pltpu.CompilerParams(vmem_limit_bytes=LIMIT),
         name="sort_blocks",
-    )(dest, count, anchor, vis, weight, pos, kernel)
+    )(in_hbm(dest), count, *map(in_hbm, (anchor, vis, weight, pos, kernel)))
 
 
 def greet_tiles(me):
@@ -139,7 +159,7 @@
     return barrier
 
 
-def route_kernel(scaled, packed, got_scaled, got_packed, s_out, s_in, p_out, p_in, here):
+def route_kernel(scaled, packed, got_scaled, got_packed, sems, here):
     me = lax.axis_index("tile")
     pl.semaphore_wait(greet_tiles(me), TILES - 1)
 
@@ -147,16 +167,16 @@
         first = pltpu.make_async_remote_copy(
             src_ref=scaled.at[pl.ds(peer * 2, 2)],
             dst_ref=got_scaled.at[pl.ds(me * 2, 2)],
-            send_sem=s_out.at[peer],
-            recv_sem=s_in.at[me],
+            send_sem=sems.at[0],
+            recv_sem=sems.at[1],
             device_id={"tile": peer},
             device_id_type=MESH,
         )
         second = pltpu.make_async_remote_copy(
             src_ref=packed.at[pl.ds(peer, 1)],
             dst_ref=got_packed.at[pl.ds(me, 1)],
-            send_sem=p_out.at[peer],
-            recv_sem=p_in.at[me],
+            send_sem=sems.at[2],
+            recv_sem=sems.at[3],
             device_id={"tile": peer},
             device_id_type=MESH,
         )
@@ -180,20 +200,10 @@
     own_scaled.wait()
     own_packed.wait()
 
-    def finish(step, carry):
-        peer = (me + step) % TILES
-        pltpu.make_async_copy(
-            got_scaled.at[pl.ds(peer * 2, 2)], got_scaled.at[pl.ds(peer * 2, 2)], s_in.at[peer]
-        ).wait()
-        pltpu.make_async_copy(
-            got_packed.at[pl.ds(peer, 1)], got_packed.at[pl.ds(peer, 1)], p_in.at[peer]
-        ).wait()
-        first, second = copies(peer)
-        first.wait_send()
-        second.wait_send()
-        return carry
-
-    lax.fori_loop(1, TILES, finish, 0)
+    most_scaled = scaled.at[pl.ds(0, SLOTS - 2)]
+    most_packed = packed.at[pl.ds(0, TILES - 1)]
+    for k, most in enumerate((most_scaled, most_scaled, most_packed, most_packed)):
+        pltpu.make_async_copy(most, most, sems.at[k]).wait()
 
 
 def route(scaled, packed):
@@ -205,7 +215,7 @@
         ),
         in_specs=[VMEM, VMEM],
         out_specs=(VMEM, VMEM),
-        scratch_shapes=[pltpu.SemaphoreType.DMA((TILES,))] * 4 + [pltpu.SemaphoreType.DMA((2,))],
+        scratch_shapes=[pltpu.SemaphoreType.DMA((4,)), pltpu.SemaphoreType.DMA((2,))],
         compiler_params=pltpu.CompilerParams(
             collective_id=0, has_side_effects=True, vmem_limit_bytes=LIMIT
         ),
@@ -481,7 +491,7 @@
 
 
 def back_kernel(
-    info, predicted, vis, summed, residual, combined, back, parts, b_out, b_in, c_out, c_in, here
+    info, predicted, vis, summed, residual, combined, back, parts, b_sems, c_out, c_in, here
 ):
     me = lax.axis_index("tile")
     chan = lax.axis_index("chan")
@@ -510,8 +520,8 @@
         return pltpu.make_async_remote_copy(
             src_ref=predicted.at[pl.ds(peer * 2, 2)],
             dst_ref=back.at[pl.ds(me * 2, 2)],
-            send_sem=b_out.at[peer],
-            recv_sem=b_in.at[me],
+            send_sem=b_sems.at[0],
+            recv_sem=b_sems.at[1],
             device_id={"tile": peer},
             device_id_type=MESH,
         )
@@ -520,9 +530,9 @@
         home((me + step) % TILES).start()
         return carry
 
+    lax.fori_loop(1, TILES, send, 0)
     for k in range(1, CHAN):
         across(k).start()
-    lax.fori_loop(1, TILES, send, 0)
     own = pltpu.make_async_copy(
         predicted.at[pl.ds(me * 2, 2)], back.at[pl.ds(me * 2, 2)], here.at[0]
     )
@@ -534,15 +544,9 @@
     combined[...] = total
     own.wait()
 
-    def finish(step, carry):
-        peer = (me + step) % TILES
-        pltpu.make_async_copy(
-            back.at[pl.ds(peer * 2, 2)], back.at[pl.ds(peer * 2, 2)], b_in.at[peer]
-        ).wait()
-        home(peer).wait_send()
-        return carry
-
-    lax.fori_loop(1, TILES, finish, 0)
+    most = predicted.at[pl.ds(0, SLOTS - 2)]
+    for k in range(2):
+        pltpu.make_async_copy(most, most, b_sems.at[k]).wait()
     for first in range(0, 16, 4):
         results = []
         for b in range(first, first + 4):
@@ -569,8 +573,7 @@
         scratch_shapes=[
             pltpu.VMEM((SLOTS, 2, 2, BLOCK), jnp.bfloat16),
             pltpu.VMEM((CHAN - 1, 2, TS // CHAN, TS), jnp.float32),
-            pltpu.SemaphoreType.DMA((TILES,)),
-            pltpu.SemaphoreType.DMA((TILES,)),
+            pltpu.SemaphoreType.DMA((2,)),
             pltpu.SemaphoreType.DMA((CHAN - 1,)),
             pltpu.SemaphoreType.DMA((CHAN - 1,)),
             pltpu.SemaphoreType.DMA((1,)),

time: 106 us -> 95.1 us (0.90)
  Pallas kernels: 98.2 us -> 92.3 us
  local copies, waits for them, and re-layouts: 5.75 us -> 1.29 us
    pallas_call x1, Pallas kernels: 38.9 us -> 33.4 us  [send_back(): pl.pallas_call(back_kernel, out_shape=(jax.ShapeDtypeStruct(vis.shape, vi...]
    unnamed x16 -> x4, local copies, waits for them, and re-layouts: 5.75 us -> 1.29 us
    pallas_call x1, Pallas kernels: 33.2 us -> 30.1 us  [route(): pl.pallas_call(route_kernel, out_shape=(jax.ShapeDtypeStruct(scaled.shape...]
    pallas_call x1, Pallas kernels: 3.56 us -> 4.86 us  [grid_blocks(): pl.pallas_call(grid_kernel, out_shape=(jax.ShapeDtypeStruct((2, 4, TS, TS...]
    pallas_call x1, Pallas kernels: 2.4 us -> 3.63 us  [degrid_blocks(): pl.pallas_call(degrid_kernel, out_shape=(jax.ShapeDtypeStruct((SLOTS, 2,...]
where the time goes in v3:
time: 95.1 us; the launch traced here: 95 us
  Pallas kernels  92.3 us (97%)
  between operations  1.34 us (1%)
  local copies, waits for them, and re-layouts  1.29 us (1%)
    pallas_call x1, Pallas kernels, send_back(): pl.pallas_call(back_kernel, out_shape=(jax.ShapeDtypeStruct(vis.shape, vi...  33.4 us
    pallas_call x1, Pallas kernels, route(): pl.pallas_call(route_kernel, out_shape=(jax.ShapeDtypeStruct(scaled.shape...  30.1 us
    pallas_call x1, Pallas kernels, join_grids(): pl.pallas_call(join_kernel, out_shape=(jax.ShapeDtypeStruct((2, 4, TS, TS...  18.2 us
    pallas_call x1, Pallas kernels, grid_blocks(): pl.pallas_call(grid_kernel, out_shape=(jax.ShapeDtypeStruct((2, 4, TS, TS...  4.86 us
    pallas_call x1, Pallas kernels, degrid_blocks(): pl.pallas_call(degrid_kernel, out_shape=(jax.ShapeDtypeStruct((SLOTS, 2,...  3.63 us
    pallas_call x1, Pallas kernels, sort_blocks(): pl.pallas_call(sort_kernel, out_shape=(jax.ShapeDtypeStruct((SLOTS, 2, 2,...  2.08 us

profile of v3, /device:TPU:1, one launch (start us, length us, event | category | flops | bytes accessed | tf_op | source)
XLA Modules:
  0.0 95.0 jit_solution(17846344694947939145)
XLA Ops:
  1.3 2.1 %sort_blocks.1 = (bf16[128,2,2,512]{3,2,1,0:T(2,128)(2,1)S(1)}, s32[64,2,512]{2,1,0:T(2,128)S(1)}, s32[16]{0:T(128)S(1)}, f32[16,128]{1,0:T(8,128)S(1)}) custom-call(s32[16]{0:T(128)} %far_dest.1, s32[1]{0:T(128)S(6)} %copy.11.count, s32[2,16]{1,0:T(2,128)} %bitcast.3, bf16[16,2,2,512]{3,2,1,0:T(2,128)(2,1)} %vis.1, bf16[16,2,512]{2,1,0:T(2,128)(2,1)} %far_weight.1, ...), custom_call_target="tpu_custom_call" | custom-call | tf_op jit(solution)/shard_map/sort_blocks/pallas_call | solution.py:124
  3.4 30.1 %route.1 = (bf16[128,2,2,512]{3,2,1,0:T(2,128)(2,1)S(1)}, s32[64,2,512]{2,1,0:T(2,128)S(1)}) custom-call(bf16[128,2,2,512]{3,2,1,0:T(2,128)(2,1)S(1)} %get-tuple-element.18.scaled, s32[64,2,512]{2,1,0:T(2,128)S(1)} %get-tuple-element.19.packed), custom_call_target="tpu_custom_call" | custom-call | tf_op jit(solution)/shard_map/route/pallas_call | solution.py:210
  33.5 4.9 %grid_blocks.1 = (f32[2,4,256,256]{3,2,1,0:T(8,128)S(1)}, s32[136]{0:T(256)S(1)}, s32[136]{0:T(256)S(1)}) custom-call(bf16[128,2,2,512]{3,2,1,0:T(2,128)(2,1)S(1)} %get-tuple-element.20.scaled, s32[64,2,512]{2,1,0:T(2,128)S(1)} %get-tuple-element.21.packed, f32[16,128]{1,0:T(8,128)S(1)} %get-tuple-element.22.table), custom_call_target="tpu_custom_call" | custom-call | tf_op jit(solution)/shard_map/grid_blocks/pallas_call | solution.py:340
  38.3 0.0 copy-start
  38.3 18.2 %join_grids.1 = (bf16[2,4,256,256]{3,2,1,0:T(8,128)(2,1)S(1)}, f32[2,256,256]{2,1,0:T(8,128)S(1)}) custom-call(f32[2,4,256,256]{3,2,1,0:T(8,128)S(1)} %get-tuple-element.25.grid), custom_call_target="tpu_custom_call" | custom-call | tf_op jit(solution)/shard_map/join_grids/pallas_call | solution.py:405
  56.6 3.6 %degrid_blocks.1 = (bf16[128,2,2,512]{3,2,1,0:T(2,128)(2,1)S(1)}, f32[2,256,256]{2,1,0:T(8,128)S(1)}) custom-call(s32[136]{0:T(256)S(1)} %get-tuple-element.23.live, s32[136]{0:T(256)S(1)} %get-tuple-element.24.words, s32[64,2,512]{2,1,0:T(2,128)S(1)} %get-tuple-element.21.packed, f32[16,128]{1,0:T(8,128)S(1)} %get-tuple-element.22.table, ...), custom_call_target="tpu_custom_call" | custom-call | tf_op jit(solution)/shard_map/degrid_blocks/pallas_call | solution.py:480
  60.2 0.0 copy-done
  60.2 33.4 %send_back.1 = (bf16[16,2,2,512]{3,2,1,0:T(2,128)(2,1)S(1)}, f32[2,64,256]{2,1,0:T(8,128)S(1)}) custom-call(s32[16]{0:T(128)S(1)} %get-tuple-element.17.info, bf16[128,2,2,512]{3,2,1,0:T(2,128)(2,1)S(1)} %get-tuple-element.28.predicted, bf16[16,2,2,512]{3,2,1,0:T(2,128)(2,1)S(1)} %copy-done, f32[2,256,256]{2,1,0:T(8,128)S(1)} %get-tuple-element.29.summed), custom_call_target="tpu_custom_call" | custom-call | tf_op jit(solution)/shard_map/send_back/pallas_call | solution.py:565
  93.7 0.7 copy.12
  94.3 0.6 copy.13
Async XLA Ops:
  38.3 21.9 %copy-start = (bf16[16,2,2,512]{3,2,1,0:T(2,128)(2,1)S(1)}, bf16[16,2,2,512]{3,2,1,0:T(2,128)(2,1)}, u32[]{:S(2)}) copy-start(bf16[16,2,2,512]{3,2,1,0:T(2,128)(2,1)} %vis.1) | copy-start | bytes 196612

commit v4 on v3

--- a/solution.py
+++ b/solution.py
@@ -17,6 +17,7 @@
 SLOTS = 128
 ROWS = 144
 GROUPS = 4
+WIDTH = 8
 LIMIT = 40 * 1024 * 1024
 
 VMEM = pl.BlockSpec(memory_space=pltpu.VMEM)
@@ -274,6 +275,10 @@
 def slot_taps(packed, table, slot, word):
     both = packed[slot >> 1]
     mine = jnp.where((slot & 1) == 1, both[1:2], both[0:1])
+    return word_taps(mine, table, word)
+
+
+def word_taps(mine, table, word):
     shift = OS * ((word >> 30) & 1)
     row_cell = (mine >> 5) & 255
     row_column = (mine & (OS - 1)) + shift
@@ -288,7 +293,7 @@
     return rows, jnp.concatenate(cols, axis=1)
 
 
-def grid_kernel(scaled, packed, table, grid, live, words, line, heads, sem):
+def grid_kernel(scaled, packed, table, grid, heads, late, line, live, sem):
     flags = jnp.concatenate([packed[:, 0, 0:128], packed[:, 1, 0:128]], axis=0)
     line[...] = jnp.broadcast_to(flags.T[0:1], (8, 128))
     fetch = pltpu.make_async_copy(line, heads, sem)
@@ -298,18 +303,23 @@
     fetch.wait()
 
     def look(device, count):
-        for which in range(2):
-            word = heads[0, which * TILES + device]
-            live[count] = device * 2 + which
-            words[count] = word
-            count = count + ((word >> 26) & 1)
-        return count
+        live[count] = device * 2
+        return count + ((heads[0, device] >> 26) & 1)
+
+    def look_late(device, counts):
+        count, extra = counts
+        live[count] = device * 2 + 1
+        late[extra] = device
+        alive = (heads[0, TILES + device] >> 26) & 1
+        return count + alive, extra + alive
 
     count = lax.fori_loop(0, TILES, look, jnp.int32(0), unroll=4)
-    live[SLOTS] = count
+    count, extra = lax.fori_loop(0, TILES, look_late, (count, jnp.int32(0)), unroll=4)
+    late[TILES] = extra
 
     def one(k, alive):
-        slot, word = live[k], words[k]
+        slot = live[k]
+        word = heads[0, (slot & 1) * TILES + (slot >> 1)]
         rows, cols = slot_taps(packed, taps, slot, word)
         keep = alive.astype(jnp.float32)
         planes = []
@@ -341,12 +351,16 @@
         grid_kernel,
         out_shape=(
             jax.ShapeDtypeStruct((2, 4, TS, TS), jnp.float32),
-            jax.ShapeDtypeStruct((SLOTS + 8,), jnp.int32),
-            jax.ShapeDtypeStruct((SLOTS + 8,), jnp.int32),
+            jax.ShapeDtypeStruct((8, 128), jnp.int32),
+            jax.ShapeDtypeStruct((TILES + 8,), jnp.int32),
         ),
         in_specs=[VMEM, VMEM, VMEM],
         out_specs=(VMEM, SMEM, SMEM),
-        scratch_shapes=[pltpu.VMEM((8, 128), jnp.int32), pltpu.SMEM((8, 128), jnp.int32), pltpu.SemaphoreType.DMA],
+        scratch_shapes=[
+            pltpu.VMEM((8, 128), jnp.int32),
+            pltpu.SMEM((SLOTS + 8,), jnp.int32),
+            pltpu.SemaphoreType.DMA,
+        ],
         compiler_params=pltpu.CompilerParams(vmem_limit_bytes=LIMIT),
         name="grid_blocks",
     )(scaled, packed, table)
@@ -441,7 +455,30 @@
     return jnp.concatenate(rows, axis=0)
 
 
-def degrid_kernel(live, words, packed, table, whole, summed, predicted, framed):
+def predict(whole, rows, cols, word):
+    rows = [jnp.concatenate(tiles, axis=0).astype(jnp.float32) for tiles in rows]
+    pair = (word >> 31) & 1
+    base = (word >> 27) & 7
+    scale = jnp.float32(1.0 / (TAPS * TAPS))
+    parts = []
+    for part in range(2):
+        results = []
+        for channel in range(2):
+            plane = part * 2 + channel
+            window = jnp.concatenate(
+                [whole[pair, plane, base + k] for k in range(ROWS // 16)], axis=0
+            )
+            across = jnp.dot(window, cols, preferred_element_type=jnp.float32)
+            sums = [
+                jnp.sum(rows[g] * across[:, g * 128 : (g + 1) * 128], axis=0, keepdims=True)
+                for g in range(GROUPS)
+            ]
+            results.append(jnp.concatenate(sums, axis=1))
+        parts.append((jnp.concatenate(results, axis=0) * scale).astype(jnp.bfloat16))
+    return parts
+
+
+def late_kernel(late, heads, packed, table, whole, summed, predicted, framed):
     upper = lax.axis_index("tile") // (TILES // 2)
     taps = table[...]
 
@@ -454,44 +491,50 @@
     def _():
         framed[...] = summed[...]
 
-    def one(k, alive):
-        slot, word = live[k], words[k]
-        rows, cols = slot_taps(packed, taps, slot, word)
-        rows = [jnp.concatenate(tiles, axis=0).astype(jnp.float32) for tiles in rows]
-        pair = (word >> 31) & 1
-        start = pl.multiple_of(((word >> 27) & 7) * 16, 16)
-        scale = jnp.float32(1.0 / (TAPS * TAPS))
-        for part in range(2):
-            results = []
-            for channel in range(2):
-                window = whole[pair, part * 2 + channel, pl.ds(start, ROWS), :]
-                across = jnp.dot(window, cols, preferred_element_type=jnp.float32)
-                sums = [
-                    jnp.sum(rows[g] * across[:, g * 128 : (g + 1) * 128], axis=0, keepdims=True)
-                    for g in range(GROUPS)
-                ]
-                results.append(jnp.concatenate(sums, axis=1))
-            predicted[slot, part] = (jnp.concatenate(results, axis=0) * scale).astype(jnp.bfloat16)
-
-    live_turns(live[SLOTS], one)
-
-
-def degrid_blocks(live, words, packed, table, whole, summed):
+    predicted[...] = jnp.zeros(predicted.shape, predicted.dtype)
+
+    def one(k, carry):
+        device = late[k]
+        word = heads[0, TILES + device]
+        rows, cols = slot_taps(packed, taps, device * 2 + 1, word)
+        for part, value in enumerate(predict(whole, rows, cols, word)):
+            predicted[device, part] = value
+        return carry
+
+    lax.fori_loop(0, late[TILES], one, 0)
+
+
+def degrid_late(late, heads, packed, table, whole, summed):
     return pl.pallas_call(
-        degrid_kernel,
+        late_kernel,
         out_shape=(
-            jax.ShapeDtypeStruct((SLOTS, 2, 2, BLOCK), jnp.bfloat16),
+            jax.ShapeDtypeStruct((TILES, 2, 2, BLOCK), jnp.bfloat16),
             jax.ShapeDtypeStruct((2, TS, TS), jnp.float32),
         ),
         in_specs=[SMEM, SMEM, VMEM, VMEM, VMEM, VMEM],
         out_specs=(VMEM, VMEM),
         compiler_params=pltpu.CompilerParams(vmem_limit_bytes=LIMIT),
-        name="degrid_blocks",
-    )(live, words, packed, table, whole, summed)
+        name="degrid_late",
+    )(late, heads, packed, table, whole, summed)
 
 
 def back_kernel(
-    info, predicted, vis, summed, residual, combined, back, parts, b_sems, c_out, c_in, here
+    info,
+    heads,
+    late,
+    packed,
+    table,
+    whole,
+    vis,
+    summed,
+    residual,
+    combined,
+    ready,
+    back,
+    parts,
+    b_sems,
+    c_out,
+    c_in,
 ):
     me = lax.axis_index("tile")
     chan = lax.axis_index("chan")
@@ -500,7 +543,7 @@
         pl.semaphore_signal(
             barrier, inc=1, device_id={"chan": (chan + k) % CHAN}, device_id_type=MESH
         )
-    pl.semaphore_wait(barrier, TILES - 1 + CHAN - 1)
+    taps = table[...]
 
     def rows_of(group):
         return pl.ds(pl.multiple_of(group * (TS // CHAN), TS // CHAN), TS // CHAN)
@@ -516,35 +559,53 @@
             device_id_type=MESH,
         )
 
+    def make(peer):
+        word = heads[0, peer]
+        both = packed[peer]
+        rows, cols = word_taps(both[0:1], taps, word)
+        for part, value in enumerate(predict(whole, rows, cols, word)):
+            ready[peer, 0, part] = value
+        ready[peer, 1] = late[peer]
+
     def home(peer):
         return pltpu.make_async_remote_copy(
-            src_ref=predicted.at[pl.ds(peer * 2, 2)],
-            dst_ref=back.at[pl.ds(me * 2, 2)],
+            src_ref=ready.at[pl.ds(peer, 1)],
+            dst_ref=back.at[pl.ds(me, 1)],
             send_sem=b_sems.at[0],
             recv_sem=b_sems.at[1],
             device_id={"tile": peer},
             device_id_type=MESH,
         )
 
-    def send(step, carry):
-        home((me + step) % TILES).start()
+    def make_group(group):
+        for k in range(WIDTH):
+            make((me + 1 + group * WIDTH + k) % TILES)
+
+    def send_group(group, width):
+        for k in range(width):
+            home((me + 1 + group * WIDTH + k) % TILES).start()
+
+    def turn(group, carry):
+        make_group(group)
+        send_group(group, WIDTH)
         return carry
 
-    lax.fori_loop(1, TILES, send, 0)
+    make_group(0)
+    pl.semaphore_wait(barrier, TILES - 1 + CHAN - 1)
+    send_group(0, WIDTH)
     for k in range(1, CHAN):
         across(k).start()
-    own = pltpu.make_async_copy(
-        predicted.at[pl.ds(me * 2, 2)], back.at[pl.ds(me * 2, 2)], here.at[0]
-    )
-    own.start()
+    last = TILES // WIDTH - 1
+    lax.fori_loop(1, last, turn, 0)
+    make_group(last)
+    send_group(last, WIDTH - 1)
+    back[me] = ready[me]
     total = summed[:, rows_of(chan), :]
     for k in range(1, CHAN):
         across(k).wait()
         total = total + parts[k - 1]
     combined[...] = total
-    own.wait()
-
-    most = predicted.at[pl.ds(0, SLOTS - 2)]
+    most = ready.at[pl.ds(0, TILES - 1)]
     for k in range(2):
         pltpu.make_async_copy(most, most, b_sems.at[k]).wait()
     for first in range(0, 16, 4):
@@ -554,35 +615,36 @@
             keep = ((word >> 9) & 1).astype(jnp.float32)
             flip = (1 - 2 * ((word >> 8) & 1)).astype(jnp.float32)
             for part in range(2):
-                value = back[word & 127, part].astype(jnp.float32)
+                value = back[(word >> 1) & 63, word & 1, part].astype(jnp.float32)
                 value = jnp.where(keep > 0.5, value * flip if part else value, jnp.float32(0.0))
                 results.append((vis[b, part].astype(jnp.float32) - value).astype(jnp.bfloat16))
         for k, result in enumerate(results):
             residual[first + k // 2, k % 2] = result
 
 
-def send_back(info, predicted, vis, summed):
+def send_back(info, heads, late, packed, table, whole, vis, summed):
+    slots = (TILES, 2, 2, 2, BLOCK)
     return pl.pallas_call(
         back_kernel,
         out_shape=(
             jax.ShapeDtypeStruct(vis.shape, vis.dtype),
             jax.ShapeDtypeStruct((2, TS // CHAN, TS), jnp.float32),
         ),
-        in_specs=[SMEM, VMEM, VMEM, VMEM],
+        in_specs=[SMEM, SMEM, VMEM, VMEM, VMEM, VMEM, VMEM, VMEM],
         out_specs=(VMEM, VMEM),
         scratch_shapes=[
-            pltpu.VMEM((SLOTS, 2, 2, BLOCK), jnp.bfloat16),
+            pltpu.VMEM(slots, jnp.bfloat16),
+            pltpu.VMEM(slots, jnp.bfloat16),
             pltpu.VMEM((CHAN - 1, 2, TS // CHAN, TS), jnp.float32),
             pltpu.SemaphoreType.DMA((2,)),
             pltpu.SemaphoreType.DMA((CHAN - 1,)),
             pltpu.SemaphoreType.DMA((CHAN - 1,)),
-            pltpu.SemaphoreType.DMA((1,)),
         ],
         compiler_params=pltpu.CompilerParams(
             collective_id=2, has_side_effects=True, vmem_limit_bytes=LIMIT
         ),
         name="send_back",
-    )(info, predicted, vis, summed)
+    )(info, heads, late, packed, table, whole, vis, summed)
 
 
 def per_device(visibility, imaging_weight, position, anchor, destination, block_count, kernel):
@@ -590,10 +652,13 @@
         destination, block_count, anchor.T, visibility, imaging_weight, position, kernel.T
     )
     scaled, packed = route(scaled, packed)
-    grid, live, words = grid_blocks(scaled, packed, table)
+    grid, heads, late = grid_blocks(scaled, packed, table)
     whole, summed = join_grids(grid)
-    predicted, framed = degrid_blocks(live, words, packed, table, whole, summed)
-    residual, combined = send_back(info, predicted, visibility, framed)
+    whole = whole.reshape(2, 4, TS // 16, 16, TS)
+    predicted, framed = degrid_late(late, heads, packed, table, whole, summed)
+    residual, combined = send_back(
+        info, heads, predicted, packed, table, whole, visibility, framed
+    )
     return combined, residual
 
 

time: 95.1 us -> 89 us (0.936)
  Pallas kernels: 92.3 us -> 86.8 us
    pallas_call x1, Pallas kernels: 33.4 us -> 30.2 us  [send_back(): pl.pallas_call(back_kernel, out_shape=(jax.ShapeDtypeStruct(vis.shape, vi...]
    pallas_call x1, Pallas kernels: 3.63 us -> 0.69 us  [degrid_late(): pl.pallas_call(late_kernel, out_shape=(jax.ShapeDtypeStruct((TILES, 2, 2,...]
where the time goes in v4:
time: 89 us; the launch traced here: 89.5 us
  Pallas kernels  86.8 us (98%)
  between operations  1.34 us (2%)
  local copies, waits for them, and re-layouts  1.29 us (1%)
    pallas_call x1, Pallas kernels, send_back(): pl.pallas_call(back_kernel, out_shape=(jax.ShapeDtypeStruct(vis.shape, vi...  30.2 us
    pallas_call x1, Pallas kernels, route(): pl.pallas_call(route_kernel, out_shape=(jax.ShapeDtypeStruct(scaled.shape...  30.1 us
    pallas_call x1, Pallas kernels, join_grids(): pl.pallas_call(join_kernel, out_shape=(jax.ShapeDtypeStruct((2, 4, TS, TS...  18.6 us
    pallas_call x1, Pallas kernels, grid_blocks(): pl.pallas_call(grid_kernel, out_shape=(jax.ShapeDtypeStruct((2, 4, TS, TS...  5.14 us
    pallas_call x1, Pallas kernels, sort_blocks(): pl.pallas_call(sort_kernel, out_shape=(jax.ShapeDtypeStruct((SLOTS, 2, 2,...  2.11 us

profile of v4, /device:TPU:1, one launch (start us, length us, event | category | flops | bytes accessed | tf_op | source)
XLA Modules:
  0.0 89.5 jit_solution(12366858202558922299)
XLA Ops:
  1.3 2.1 %sort_blocks.1 = (bf16[128,2,2,512]{3,2,1,0:T(2,128)(2,1)S(1)}, s32[64,2,512]{2,1,0:T(2,128)S(1)}, s32[16]{0:T(128)S(1)}, f32[16,128]{1,0:T(8,128)S(1)}) custom-call(s32[16]{0:T(128)} %far_dest.1, s32[1]{0:T(128)S(6)} %copy.11.count, s32[2,16]{1,0:T(2,128)} %bitcast.6, bf16[16,2,2,512]{3,2,1,0:T(2,128)(2,1)} %vis.1, bf16[16,2,512]{2,1,0:T(2,128)(2,1)} %far_weight.1, ...), custom_call_target="tpu_custom_call" | custom-call | tf_op jit(solution)/shard_map/sort_blocks/pallas_call | solution.py:125
  3.4 30.1 %route.1 = (bf16[128,2,2,512]{3,2,1,0:T(2,128)(2,1)S(1)}, s32[64,2,512]{2,1,0:T(2,128)S(1)}) custom-call(bf16[128,2,2,512]{3,2,1,0:T(2,128)(2,1)S(1)} %get-tuple-element.18.scaled, s32[64,2,512]{2,1,0:T(2,128)S(1)} %get-tuple-element.19.packed), custom_call_target="tpu_custom_call" | custom-call | tf_op jit(solution)/shard_map/route/pallas_call | solution.py:211
  33.5 5.1 %grid_blocks.1 = (f32[2,4,256,256]{3,2,1,0:T(8,128)S(1)}, s32[8,128]{1,0:T(8,128)S(1)}, s32[72]{0:T(128)S(1)}) custom-call(bf16[128,2,2,512]{3,2,1,0:T(2,128)(2,1)S(1)} %get-tuple-element.20.scaled, s32[64,2,512]{2,1,0:T(2,128)S(1)} %get-tuple-element.21.packed, f32[16,128]{1,0:T(8,128)S(1)} %get-tuple-element.22.table), custom_call_target="tpu_custom_call" | custom-call | tf_op jit(solution)/shard_map/grid_blocks/pallas_call | solution.py:350
  38.6 0.0 copy-start
  38.7 18.6 %join_grids.1 = (bf16[2,4,256,256]{3,2,1,0:T(8,128)(2,1)S(1)}, f32[2,256,256]{2,1,0:T(8,128)S(1)}) custom-call(f32[2,4,256,256]{3,2,1,0:T(8,128)S(1)} %get-tuple-element.25.grid), custom_call_target="tpu_custom_call" | custom-call | tf_op jit(solution)/shard_map/join_grids/pallas_call | solution.py:419
  57.3 0.7 degrid_late.1
  58.0 0.0 copy-done
  58.0 30.2 %send_back.1 = (bf16[16,2,2,512]{3,2,1,0:T(2,128)(2,1)S(1)}, f32[2,64,256]{2,1,0:T(8,128)S(1)}) custom-call(s32[16]{0:T(128)S(1)} %get-tuple-element.17.info, s32[8,128]{1,0:T(8,128)S(1)} %get-tuple-element.23.heads, bf16[64,2,2,512]{3,2,1,0:T(2,128)(2,1)S(1)} %get-tuple-element.28.late, s32[64,2,512]{2,1,0:T(2,128)S(1)} %get-tuple-element.21.packed, ...), custom_call_target="tpu_custom_call" | custom-call | tf_op jit(solution)/shard_map/send_back/pallas_call | solution.py:627
  88.2 0.7 copy.12
  88.8 0.6 copy.13
Async XLA Ops:
  38.6 19.4 %copy-start = (bf16[16,2,2,512]{3,2,1,0:T(2,128)(2,1)S(1)}, bf16[16,2,2,512]{3,2,1,0:T(2,128)(2,1)}, u32[]{:S(2)}) copy-start(bf16[16,2,2,512]{3,2,1,0:T(2,128)(2,1)} %vis.1) | copy-start | bytes 196612

commit v5 on v4

--- a/solution.py
+++ b/solution.py
@@ -18,7 +18,7 @@
 ROWS = 144
 GROUPS = 4
 WIDTH = 8
-LIMIT = 40 * 1024 * 1024
+LIMIT = 16 * 1024 * 1024
 
 VMEM = pl.BlockSpec(memory_space=pltpu.VMEM)
 SMEM = pl.BlockSpec(memory_space=pltpu.SMEM)
@@ -160,12 +160,12 @@
     return barrier
 
 
-def route_kernel(scaled, packed, got_scaled, got_packed, sems, here):
+def route_kernel(scaled, packed, table, got_scaled, got_packed, row_taps, col_taps, sems, here):
     me = lax.axis_index("tile")
     pl.semaphore_wait(greet_tiles(me), TILES - 1)
 
-    def copies(peer):
-        first = pltpu.make_async_remote_copy(
+    def values_copy(peer):
+        return pltpu.make_async_remote_copy(
             src_ref=scaled.at[pl.ds(peer * 2, 2)],
             dst_ref=got_scaled.at[pl.ds(me * 2, 2)],
             send_sem=sems.at[0],
@@ -173,7 +173,9 @@
             device_id={"tile": peer},
             device_id_type=MESH,
         )
-        second = pltpu.make_async_remote_copy(
+
+    def places_copy(peer):
+        return pltpu.make_async_remote_copy(
             src_ref=packed.at[pl.ds(peer, 1)],
             dst_ref=got_packed.at[pl.ds(me, 1)],
             send_sem=sems.at[2],
@@ -181,15 +183,17 @@
             device_id={"tile": peer},
             device_id_type=MESH,
         )
-        return first, second
-
-    def send(step, carry):
-        first, second = copies((me + step) % TILES)
-        first.start()
-        second.start()
+
+    def send_places(step, carry):
+        places_copy((me + step) % TILES).start()
         return carry
 
-    lax.fori_loop(1, TILES, send, 0)
+    def send_values(step, carry):
+        values_copy((me + step) % TILES).start()
+        return carry
+
+    lax.fori_loop(1, TILES, send_places, 0)
+    lax.fori_loop(1, TILES, send_values, 0)
     own_scaled = pltpu.make_async_copy(
         scaled.at[pl.ds(me * 2, 2)], got_scaled.at[pl.ds(me * 2, 2)], here.at[0]
     )
@@ -203,25 +207,42 @@
 
     most_scaled = scaled.at[pl.ds(0, SLOTS - 2)]
     most_packed = packed.at[pl.ds(0, TILES - 1)]
-    for k, most in enumerate((most_scaled, most_scaled, most_packed, most_packed)):
+    pltpu.make_async_copy(most_packed, most_packed, sems.at[3]).wait()
+    taps = table[...]
+
+    def build(group, carry):
+        for k in range(4):
+            device = group * 4 + k
+            places = got_packed[device]
+            rows, cols = word_taps(places[0:1], taps, (places[0:1, 0:128] >> 30) & 1)
+            row_taps[device] = jnp.concatenate(
+                [jnp.concatenate(tiles, axis=0) for tiles in rows], axis=1
+            )
+            col_taps[device] = cols
+        return carry
+
+    lax.fori_loop(0, TILES // 4, build, 0)
+    for k, most in enumerate((most_scaled, most_scaled, most_packed)):
         pltpu.make_async_copy(most, most, sems.at[k]).wait()
 
 
-def route(scaled, packed):
+def route(scaled, packed, table):
     return pl.pallas_call(
         route_kernel,
         out_shape=(
             jax.ShapeDtypeStruct(scaled.shape, scaled.dtype),
             jax.ShapeDtypeStruct(packed.shape, packed.dtype),
-        ),
-        in_specs=[VMEM, VMEM],
-        out_specs=(VMEM, VMEM),
+            jax.ShapeDtypeStruct((TILES, ROWS, BLOCK), jnp.bfloat16),
+            jax.ShapeDtypeStruct((TILES, TS, BLOCK), jnp.bfloat16),
+        ),
+        in_specs=[VMEM, VMEM, VMEM],
+        out_specs=(VMEM, VMEM, VMEM, VMEM),
         scratch_shapes=[pltpu.SemaphoreType.DMA((4,)), pltpu.SemaphoreType.DMA((2,))],
         compiler_params=pltpu.CompilerParams(
             collective_id=0, has_side_effects=True, vmem_limit_bytes=LIMIT
         ),
         name="route",
-    )(scaled, packed)
+    )(scaled, packed, table)
 
 
 def live_turns(count, one):
@@ -275,11 +296,13 @@
 def slot_taps(packed, table, slot, word):
     both = packed[slot >> 1]
     mine = jnp.where((slot & 1) == 1, both[1:2], both[0:1])
-    return word_taps(mine, table, word)
-
-
-def word_taps(mine, table, word):
-    shift = OS * ((word >> 30) & 1)
+    return word_taps(mine, table, (word >> 30) & 1)
+
+
+def word_taps(mine, table, mirror):
+    shift = OS * mirror
+    if getattr(mirror, "shape", ()):
+        shift = jnp.concatenate([shift] * GROUPS, axis=1)
     row_cell = (mine >> 5) & 255
     row_column = (mine & (OS - 1)) + shift
     col_cell = (mine >> 18) & 255
@@ -293,7 +316,7 @@
     return rows, jnp.concatenate(cols, axis=1)
 
 
-def grid_kernel(scaled, packed, table, grid, heads, late, line, live, sem):
+def grid_kernel(scaled, packed, table, row_taps, col_taps, grid, heads, late, line, live, sem):
     flags = jnp.concatenate([packed[:, 0, 0:128], packed[:, 1, 0:128]], axis=0)
     line[...] = jnp.broadcast_to(flags.T[0:1], (8, 128))
     fetch = pltpu.make_async_copy(line, heads, sem)
@@ -302,25 +325,33 @@
     taps = table[...]
     fetch.wait()
 
-    def look(device, count):
-        live[count] = device * 2
-        return count + ((heads[0, device] >> 26) & 1)
-
-    def look_late(device, counts):
+    def look(device, counts):
         count, extra = counts
-        live[count] = device * 2 + 1
+        live[count] = device
         late[extra] = device
-        alive = (heads[0, TILES + device] >> 26) & 1
-        return count + alive, extra + alive
-
-    count = lax.fori_loop(0, TILES, look, jnp.int32(0), unroll=4)
-    count, extra = lax.fori_loop(0, TILES, look_late, (count, jnp.int32(0)), unroll=4)
+        return count + ((heads[0, device] >> 26) & 1), extra + (
+            (heads[0, TILES + device] >> 26) & 1
+        )
+
+    count, extra = lax.fori_loop(0, TILES, look, (jnp.int32(0), jnp.int32(0)), unroll=4)
     late[TILES] = extra
 
     def one(k, alive):
-        slot = live[k]
-        word = heads[0, (slot & 1) * TILES + (slot >> 1)]
-        rows, cols = slot_taps(packed, taps, slot, word)
+        device = live[k]
+        rows = row_taps[device]
+        rows = [
+            [rows[m * 16 : m * 16 + 16, g * 128 : g * 128 + 128] for m in range(ROWS // 16)]
+            for g in range(GROUPS)
+        ]
+        add(device * 2, heads[0, device], alive, rows, col_taps[device])
+
+    def one_late(k, carry):
+        device = late[k]
+        slot, word = device * 2 + 1, heads[0, TILES + device]
+        add(slot, word, jnp.bool_(True), *slot_taps(packed, taps, slot, word))
+        return carry
+
+    def add(slot, word, alive, rows, cols):
         keep = alive.astype(jnp.float32)
         planes = []
         for part in range(2):
@@ -344,9 +375,10 @@
             grid[pair, plane, pl.ds(start, ROWS), :] += product[plane * ROWS : (plane + 1) * ROWS]
 
     live_turns(count, one)
-
-
-def grid_blocks(scaled, packed, table):
+    lax.fori_loop(0, extra, one_late, 0)
+
+
+def grid_blocks(scaled, packed, table, row_taps, col_taps):
     return pl.pallas_call(
         grid_kernel,
         out_shape=(
@@ -354,7 +386,7 @@
             jax.ShapeDtypeStruct((8, 128), jnp.int32),
             jax.ShapeDtypeStruct((TILES + 8,), jnp.int32),
         ),
-        in_specs=[VMEM, VMEM, VMEM],
+        in_specs=[VMEM, VMEM, VMEM, VMEM, VMEM],
         out_specs=(VMEM, SMEM, SMEM),
         scratch_shapes=[
             pltpu.VMEM((8, 128), jnp.int32),
@@ -363,7 +395,7 @@
         ],
         compiler_params=pltpu.CompilerParams(vmem_limit_bytes=LIMIT),
         name="grid_blocks",
-    )(scaled, packed, table)
+    )(scaled, packed, table, row_taps, col_taps)
 
 
 def join_kernel(grid, whole, summed, half, got_half, total, mine, got_mine, send, recv):
@@ -385,12 +417,13 @@
             device_id_type=MESH,
         )
 
+    for k in range(4):
+        half[k] = grid[1 - core, k].astype(jnp.bfloat16)
     pl.semaphore_wait(barrier, 2)
     first = [pass_on(half.at[k], got_half.at[k], k, near) for k in range(4)]
     second = [pass_on(mine.at[k], got_mine.at[k], 4 + k, far) for k in range(4)]
     third = [pass_on(whole.at[core, k], whole.at[core, k], 8 + k, near) for k in range(4)]
     for k in range(4):
-        half[k] = grid[1 - core, k].astype(jnp.bfloat16)
         first[k].start()
     for k in range(4):
         first[k].wait_recv()
@@ -456,7 +489,6 @@
 
 
 def predict(whole, rows, cols, word):
-    rows = [jnp.concatenate(tiles, axis=0).astype(jnp.float32) for tiles in rows]
     pair = (word >> 31) & 1
     base = (word >> 27) & 7
     scale = jnp.float32(1.0 / (TAPS * TAPS))
@@ -497,6 +529,7 @@
         device = late[k]
         word = heads[0, TILES + device]
         rows, cols = slot_taps(packed, taps, device * 2 + 1, word)
+        rows = [jnp.concatenate(tiles, axis=0).astype(jnp.float32) for tiles in rows]
         for part, value in enumerate(predict(whole, rows, cols, word)):
             predicted[device, part] = value
         return carry
@@ -522,8 +555,8 @@
     info,
     heads,
     late,
-    packed,
-    table,
+    row_taps,
+    col_taps,
     whole,
     vis,
     summed,
@@ -543,7 +576,6 @@
         pl.semaphore_signal(
             barrier, inc=1, device_id={"chan": (chan + k) % CHAN}, device_id_type=MESH
         )
-    taps = table[...]
 
     def rows_of(group):
         return pl.ds(pl.multiple_of(group * (TS // CHAN), TS // CHAN), TS // CHAN)
@@ -560,10 +592,9 @@
         )
 
     def make(peer):
-        word = heads[0, peer]
-        both = packed[peer]
-        rows, cols = word_taps(both[0:1], taps, word)
-        for part, value in enumerate(predict(whole, rows, cols, word)):
+        rows = row_taps[peer].astype(jnp.float32)
+        rows = [rows[:, g * 128 : g * 128 + 128] for g in range(GROUPS)]
+        for part, value in enumerate(predict(whole, rows, col_taps[peer], heads[0, peer])):
             ready[peer, 0, part] = value
         ready[peer, 1] = late[peer]
 
@@ -622,7 +653,7 @@
             residual[first + k // 2, k % 2] = result
 
 
-def send_back(info, heads, late, packed, table, whole, vis, summed):
+def send_back(info, heads, late, row_taps, col_taps, whole, vis, summed):
     slots = (TILES, 2, 2, 2, BLOCK)
     return pl.pallas_call(
         back_kernel,
@@ -644,20 +675,20 @@
             collective_id=2, has_side_effects=True, vmem_limit_bytes=LIMIT
         ),
         name="send_back",
-    )(info, heads, late, packed, table, whole, vis, summed)
+    )(info, heads, late, row_taps, col_taps, whole, vis, summed)
 
 
 def per_device(visibility, imaging_weight, position, anchor, destination, block_count, kernel):
     scaled, packed, info, table = sort_blocks(
         destination, block_count, anchor.T, visibility, imaging_weight, position, kernel.T
     )
-    scaled, packed = route(scaled, packed)
-    grid, heads, late = grid_blocks(scaled, packed, table)
+    scaled, packed, row_taps, col_taps = route(scaled, packed, table)
+    grid, heads, late = grid_blocks(scaled, packed, table, row_taps, col_taps)
     whole, summed = join_grids(grid)
     whole = whole.reshape(2, 4, TS // 16, 16, TS)
     predicted, framed = degrid_late(late, heads, packed, table, whole, summed)
     residual, combined = send_back(
-        info, heads, predicted, packed, table, whole, visibility, framed
+        info, heads, predicted, row_taps, col_taps, whole, visibility, framed
     )
     return combined, residual
 

time: 89 us -> 87.9 us (0.988)
    pallas_call x1, Pallas kernels: 5.14 us -> 4.14 us  [grid_blocks(): pl.pallas_call(grid_kernel, out_shape=(jax.ShapeDtypeStruct((2, 4, TS, TS...]
where the time goes in v5:
time: 87.9 us; the launch traced here: 89 us
  Pallas kernels  86.3 us (98%)
  between operations  1.34 us (2%)
  local copies, waits for them, and re-layouts  1.29 us (1%)
    pallas_call x1, Pallas kernels, send_back(): pl.pallas_call(back_kernel, out_shape=(jax.ShapeDtypeStruct(vis.shape, vi...  30.6 us
    pallas_call x1, Pallas kernels, route(): pl.pallas_call(route_kernel, out_shape=(jax.ShapeDtypeStruct(scaled.shape...  30.2 us
    pallas_call x1, Pallas kernels, join_grids(): pl.pallas_call(join_kernel, out_shape=(jax.ShapeDtypeStruct((2, 4, TS, TS...  18.6 us
    pallas_call x1, Pallas kernels, grid_blocks(): pl.pallas_call(grid_kernel, out_shape=(jax.ShapeDtypeStruct((2, 4, TS, TS...  4.14 us
    pallas_call x1, Pallas kernels, sort_blocks(): pl.pallas_call(sort_kernel, out_shape=(jax.ShapeDtypeStruct((SLOTS, 2, 2,...  2.09 us

profile of v5, /device:TPU:1, one launch (start us, length us, event | category | flops | bytes accessed | tf_op | source)
XLA Modules:
  0.0 89.0 jit_solution(1396084280635420226)
XLA Ops:
  1.3 2.1 %sort_blocks.1 = (bf16[128,2,2,512]{3,2,1,0:T(2,128)(2,1)S(1)}, s32[64,2,512]{2,1,0:T(2,128)S(1)}, s32[16]{0:T(128)S(1)}, f32[16,128]{1,0:T(8,128)S(1)}) custom-call(s32[16]{0:T(128)} %far_dest.1, s32[1]{0:T(128)S(6)} %copy.11.count, s32[2,16]{1,0:T(2,128)} %bitcast.6, bf16[16,2,2,512]{3,2,1,0:T(2,128)(2,1)} %vis.1, bf16[16,2,512]{2,1,0:T(2,128)(2,1)} %far_weight.1, ...), custom_call_target="tpu_custom_call" | custom-call | tf_op jit(solution)/shard_map/sort_blocks/pallas_call | solution.py:125
  3.4 30.2 %route.1 = (bf16[128,2,2,512]{3,2,1,0:T(2,128)(2,1)S(1)}, s32[64,2,512]{2,1,0:T(2,128)S(1)}, bf16[64,144,512]{2,1,0:T(8,128)(2,1)S(1)}, bf16[64,256,512]{2,1,0:T(8,128)(2,1)S(1)}) custom-call(bf16[128,2,2,512]{3,2,1,0:T(2,128)(2,1)S(1)} %get-tuple-element.20.scaled, s32[64,2,512]{2,1,0:T(2,128)S(1)} %get-tuple-element.21.packed, ...), custom_call_target="tpu_custom_call" | custom-call | tf_op jit(solution)/shard_map/route/pallas_call | solution.py:230
  33.6 0.0 copy-start
  33.6 4.1 %grid_blocks.1 = (f32[2,4,256,256]{3,2,1,0:T(8,128)S(1)}, s32[8,128]{1,0:T(8,128)S(1)}, s32[72]{0:T(128)S(1)}) custom-call(bf16[128,2,2,512]{3,2,1,0:T(2,128)(2,1)S(1)} %get-tuple-element.23.scaled, s32[64,2,512]{2,1,0:T(2,128)S(1)} %get-tuple-element.24.packed, f32[16,128]{1,0:T(8,128)S(1)} %get-tuple-element.22.table, ...), custom_call_target="tpu_custom_call" | custom-call | tf_op jit(solution)/shard_map/grid_blocks/pallas_call | solution.py:382
  37.8 18.6 %join_grids.1 = (bf16[2,4,256,256]{3,2,1,0:T(8,128)(2,1)S(1)}, f32[2,256,256]{2,1,0:T(8,128)S(1)}) custom-call(f32[2,4,256,256]{3,2,1,0:T(8,128)S(1)} %get-tuple-element.29.grid), custom_call_target="tpu_custom_call" | custom-call | tf_op jit(solution)/shard_map/join_grids/pallas_call | solution.py:452
  56.4 0.7 degrid_late.1
  57.1 0.0 copy-done
  57.1 30.6 %send_back.1 = (bf16[16,2,2,512]{3,2,1,0:T(2,128)(2,1)S(1)}, f32[2,64,256]{2,1,0:T(8,128)S(1)}) custom-call(s32[16]{0:T(128)S(1)} %get-tuple-element.19.info, s32[8,128]{1,0:T(8,128)S(1)} %get-tuple-element.27.heads, bf16[64,2,2,512]{3,2,1,0:T(2,128)(2,1)S(1)} %get-tuple-element.32.late, bf16[64,144,512]{2,1,0:T(8,128)(2,1)S(1)} %get-tuple-element.25.row_taps, ...), custom_call_target="tpu_custom_call" | custom-call | tf_op jit(solution)/shard_map/send_back/pallas_call | solution.py:658
  87.7 0.7 copy.12
  88.3 0.6 copy.13
Async XLA Ops:
  33.6 23.5 %copy-start = (bf16[16,2,2,512]{3,2,1,0:T(2,128)(2,1)S(1)}, bf16[16,2,2,512]{3,2,1,0:T(2,128)(2,1)}, u32[]{:S(2)}) copy-start(bf16[16,2,2,512]{3,2,1,0:T(2,128)(2,1)} %vis.1) | copy-start | bytes 196612
